TPU v7x, 1024 devices: a whole 4x4x32 slice. The times are simulated.
1024 devices in a mesh: grp: 64 (over z, core), tile: 16 (over x, y).
Axes of the slice: x: 4, y: 4, z: 32, core: 2. Of those that a mesh axis runs over, the one named last changes fastest.
Arguments:
- pair_rep: bfloat16 [64, 96, 96, 128], P('grp', 'tile'), may hold values from -6 to 6
- cotangent: bfloat16 [64, 96, 96, 128], P('grp', 'tile'), may hold values from -6 to 6
- lengths: int32 [64], P('grp'), may hold values from 48 to 96, as said below
- in_gain: float32 [128], replicated, may hold values from 0.1 to 1.9
- projections: bfloat16 [128, 512], replicated, may hold values from -0.5 to 0.5
- gate_weight: bfloat16 [128, 128], replicated, may hold values from -0.5 to 0.5
- out_gain: float32 [128], replicated, may hold values from 0.1 to 1.9
- out_weight: bfloat16 [128, 128], replicated, may hold values from -0.5 to 0.5
Outputs:
- pair_out: bfloat16 [64, 96, 96, 128], P('grp', 'tile')
- pair_grad: bfloat16 [64, 96, 96, 128], P('grp', 'tile')
- proj_grad: float32 [128, 512], replicated
- gate_grad: float32 [128, 128], replicated
- out_weight_grad: float32 [128, 128], replicated
- in_gain_grad: float32 [128], replicated
- out_gain_grad: float32 [128], replicated
Inputs may be any that keep to these rules, and one draw needn't show every extreme that they name: `lengths`: entries of a complex whose row or column residue is at or beyond its crop length are masked; some crop has all 96 residues.
All inputs are finite; a program needn't handle non-finite values.
Results may differ from a plain program's by a relative error of at most 0.0094.
Values may be sent and summed in bfloat16 or wider, within the bound.
No kernel may reach another device: no remote copies, remote signals or barrier semaphores. Data moves between devices by JAX's collectives and lax.ppermute only.
A program may use at most 32 MiB of HBM per device.

v0:
```python
import jax
import jax.numpy as jnp
from jax import lax
from jax.sharding import PartitionSpec as P


def normalize(values, gain):
    centred = values - jnp.mean(values, axis=-1, keepdims=True)
    inverse = lax.rsqrt(jnp.mean(centred * centred, axis=-1, keepdims=True) + 1e-05)
    scaled = centred * inverse
    return (scaled, inverse, scaled * gain)


def norm_back(upstream, scaled, inverse, gain):
    grad_scaled = upstream * gain
    first_mean = jnp.mean(grad_scaled, axis=-1, keepdims=True)
    second_mean = jnp.mean(grad_scaled * scaled, axis=-1, keepdims=True)
    return inverse * (grad_scaled - first_mean - scaled * second_mean)


def body(pair_rep, cotangent, lengths, in_gain, projections, gate_weight, out_gain, out_weight):
    row_count = pair_rep.shape[1]
    residues = pair_rep.shape[2]
    chans = pair_rep.shape[3]
    width = projections.shape[1] // 4
    first_row = lax.axis_index("tile") * row_count
    col_mask = (jnp.arange(residues) < lengths[0]).astype(jnp.float32)
    row_mask = lax.dynamic_slice_in_dim(col_mask, first_row, row_count)
    pair_mask = row_mask[:, None, None] * col_mask[None, :, None]
    values = pair_rep[0].astype(jnp.float32)
    scaled_in, inverse_in, normed = normalize(values, in_gain)
    normed_in = normed.astype(jnp.bfloat16)
    linear = jnp.dot(normed_in, projections, preferred_element_type=jnp.float32)
    lin_left = linear[..., :width]
    sig_left = jax.nn.sigmoid(linear[..., width : 2 * width])
    lin_right = linear[..., 2 * width : 3 * width]
    sig_right = jax.nn.sigmoid(linear[..., 3 * width :])
    gate_lin = jnp.dot(normed_in, gate_weight, preferred_element_type=jnp.float32)
    left_panel = (sig_left * lin_left * pair_mask).astype(jnp.bfloat16)
    right_panel = (sig_right * lin_right * pair_mask).astype(jnp.bfloat16)
    left_flip = jnp.transpose(left_panel, (2, 0, 1))
    right_flip = jnp.transpose(right_panel, (2, 0, 1))
    left_chan, right_chan = (
        lax.all_to_all(left_flip, "tile", split_axis=0, concat_axis=1, tiled=True),
        lax.all_to_all(right_flip, "tile", split_axis=0, concat_axis=1, tiled=True),
    )
    tri_chan = jnp.einsum(
        "hik,hjk->hij", left_chan, right_chan, preferred_element_type=jnp.float32
    ).astype(jnp.bfloat16)
    tri_rows = lax.all_to_all(tri_chan, "tile", split_axis=1, concat_axis=0, tiled=True)
    triangle = jnp.transpose(tri_rows, (1, 2, 0)).astype(jnp.float32)
    scaled_out, inverse_out, normed_o = normalize(triangle, out_gain)
    normed_out = normed_o.astype(jnp.bfloat16)
    update = jnp.dot(normed_out, out_weight, preferred_element_type=jnp.float32)
    gate_sig = jax.nn.sigmoid(gate_lin)
    pair_out = (values + gate_sig * update).astype(jnp.bfloat16)
    upstream = cotangent[0].astype(jnp.float32)
    grad_update = (gate_sig * upstream).astype(jnp.bfloat16)
    grad_gate = (upstream * update * gate_sig * (1.0 - gate_sig)).astype(jnp.bfloat16)
    flat_out = normed_out.reshape(-1, width)
    flat_in = normed_in.reshape(-1, chans)
    out_weight_grad = jnp.dot(
        flat_out.T, grad_update.reshape(-1, chans), preferred_element_type=jnp.float32
    )
    gate_grad = jnp.dot(flat_in.T, grad_gate.reshape(-1, chans), preferred_element_type=jnp.float32)
    grad_normed_out = jnp.dot(grad_update, out_weight.T, preferred_element_type=jnp.float32)
    out_gain_grad = jnp.sum(grad_normed_out * scaled_out, axis=(0, 1))
    grad_tri = norm_back(grad_normed_out, scaled_out, inverse_out, out_gain).astype(jnp.bfloat16)
    grad_flip = jnp.transpose(grad_tri, (2, 0, 1))
    grad_chan = lax.all_to_all(grad_flip, "tile", split_axis=0, concat_axis=1, tiled=True)
    left_again, right_again = (left_chan, right_chan)
    left_back = jnp.einsum(
        "hij,hjk->hik", grad_chan, right_again, preferred_element_type=jnp.float32
    ).astype(jnp.bfloat16)
    right_back = jnp.einsum(
        "hij,hik->hjk", grad_chan, left_again, preferred_element_type=jnp.float32
    ).astype(jnp.bfloat16)
    left_rows, right_rows = (
        lax.all_to_all(left_back, "tile", split_axis=1, concat_axis=0, tiled=True),
        lax.all_to_all(right_back, "tile", split_axis=1, concat_axis=0, tiled=True),
    )
    left_grad = jnp.transpose(left_rows, (1, 2, 0)).astype(jnp.float32)
    right_grad = jnp.transpose(right_rows, (1, 2, 0)).astype(jnp.float32)
    grad_lin = jnp.concatenate(
        [
            (left_grad * sig_left * pair_mask).astype(jnp.bfloat16),
            (left_grad * lin_left * pair_mask * sig_left * (1.0 - sig_left)).astype(jnp.bfloat16),
            (right_grad * sig_right * pair_mask).astype(jnp.bfloat16),
            (right_grad * lin_right * pair_mask * sig_right * (1.0 - sig_right)).astype(
                jnp.bfloat16
            ),
        ],
        axis=-1,
    )
    proj_grad = jnp.dot(
        flat_in.T, grad_lin.reshape(-1, 4 * width), preferred_element_type=jnp.float32
    )
    grad_normed_in = jnp.dot(grad_lin, projections.T, preferred_element_type=jnp.float32) + jnp.dot(
        grad_gate, gate_weight.T, preferred_element_type=jnp.float32
    )
    in_gain_grad = jnp.sum(grad_normed_in * scaled_in, axis=(0, 1))
    pair_grad = (upstream + norm_back(grad_normed_in, scaled_in, inverse_in, in_gain)).astype(
        jnp.bfloat16
    )
    summed = lax.psum(
        (proj_grad, gate_grad, out_weight_grad, in_gain_grad, out_gain_grad), ("grp", "tile")
    )
    return (pair_out[None], pair_grad[None], summed[0], summed[1], summed[2], summed[3], summed[4])


def solution(mesh):
    return jax.shard_map(
        body,
        mesh=mesh,
        in_specs=(
            P("grp", "tile", None, None),
            P("grp", "tile", None, None),
            P("grp"),
            P(),
            P(),
            P(),
            P(),
            P(),
        ),
        out_specs=(
            P("grp", "tile", None, None),
            P("grp", "tile", None, None),
            P(),
            P(),
            P(),
            P(),
            P(),
        ),
        check_vma=False,
    )
```

profile of v0, /device:TPU:1, one launch (start us, length us, event | category | flops | bytes accessed | tf_op | source)
XLA Modules:
  0.0 1145.6 jit_solution(4061714986909923090)
XLA Ops:
  7.9 0.1 dynamic_slice.3
  8.0 1.0 convert_reduce_fusion
  9.1 1.2 fusion.16
  10.3 1.3 fusion.54
  11.6 0.2 fusion.48
  11.8 0.9 copy.44
  12.7 7.6 all-to-all-start
  20.3 0.9 copy.47
  21.1 6.4 all-to-all-done
  27.6 3.5 all-to-all-start.1
  31.2 8.3 all-to-all-done.1
  39.5 0.2 convolution_convert_fusion.2
  39.8 0.8 copy.52
  40.5 3.5 all-to-all-start.2
  44.1 0.3 fusion.2
  44.5 7.7 all-to-all-done.2
  52.3 0.2 copy.54
  52.4 0.2 bitcast_reduce_fusion
  52.6 0.3 multiply_reduce_fusion.2
  53.0 1.0 fusion.21
  54.0 0.5 multiply_reduce_fusion
  54.5 1.0 convolution_bitcast_fusion.2
  55.5 0.4 fusion.42
  55.9 0.9 copy.56
  56.8 3.5 all-to-all-start.3
  60.3 1.0 convolution_bitcast_fusion.1
  61.3 6.2 all-to-all-done.3
  67.6 0.2 copy.64
  67.8 0.2 convolution_convert_fusion
  68.0 0.7 copy.66
  68.8 3.5 all-to-all-start.5
  72.3 0.3 convolution_convert_fusion.1
  72.6 0.8 copy.61
  73.3 6.0 all-to-all-done.5
  79.3 3.6 all-to-all-start.4
  83.0 0.2 copy.68
  83.2 6.7 all-to-all-done.4
  89.9 0.2 copy.63
  90.1 0.3 fusion.36
  90.4 1.3 convolution_bitcast_fusion
  91.7 0.3 fusion.52
  92.0 0.5 fusion.15
  92.5 171.2 %all-reduce = (f32[128]{0:T(128)}, f32[128]{0:T(128)}) all-reduce(f32[128]{0:T(128)S(1)} %get-tuple-element.9, f32[128]{0:T(128)S(1)} %get-tuple-element.7), channel_id=1, replica_groups=mesh['grp'=64,'tile'=16] {'grp','tile'}, use_global_device_ids=true, to_apply=%region_12.0 | all-reduce | flops 256 | bytes 2048 | tf_op jit(solution)/shard_map/psum | solution.py:105
  263.7 1.0 fusion.50
  264.7 869.5 %all-reduce.4.cloned.1.call-done = (f32[128,512]{1,0:T(8,128)}, f32[128,128]{1,0:T(8,128)}, f32[128,128]{1,0:T(8,128)}) async-done(((f32[128,512]{1,0:T(8,128)}, f32[128,128]{1,0:T(8,128)}, f32[128,128]{1,0:T(8,128)}), (f32[128,512]{1,0:T(8,128)}, f32[128,128]{1,0:T(8,128)}, f32[128,128]{1,0:T(8,128)})) %all-reduce.4.cloned.1.call-update) | async-done | bytes 393232 | tf_op jit(solution)/shard_map/psum | solution.py:105
  1134.2 1.7 copy.87
  1135.9 1.5 copy.88
  1137.3 1.5 copy.89
  (31 shorter events, 0.4 us)
Async XLA Ops:
  7.2 3.1 copy-start
  12.7 14.9 %all-to-all-start = ((bf16[128,6,96]{2,1,0:T(8,128)(2,1)}), bf16[128,6,96]{2,1,0:T(8,128)(2,1)S(1)}, u32[]{:S(2)}, u32[]{:S(2)}) async-start(bf16[128,6,96]{2,1,0:T(8,128)(2,1)} %copy.44), calls=%async_computation | async-start | bytes 524288 | tf_op jit(solution)/shard_map/all_to_all | solution.py:44
  27.6 11.9 %all-to-all-start.1 = ((bf16[128,6,96]{2,1,0:T(8,128)(2,1)}), bf16[128,6,96]{2,1,0:T(8,128)(2,1)S(1)}, u32[]{:S(2)}, u32[]{:S(2)}) async-start(bf16[128,6,96]{2,1,0:T(8,128)(2,1)} %copy.47), calls=%async_computation.1 | async-start | bytes 524288 | tf_op jit(solution)/shard_map/all_to_all | solution.py:45
  31.1 13.0 %copy-start.1 = (bf16[1,6,96,128]{3,2,1,0:T(8,128)(2,1)S(1)}, bf16[1,6,96,128]{3,2,1,0:T(8,128)(2,1)}, u32[]{:S(2)}) copy-start(bf16[1,6,96,128]{3,2,1,0:T(8,128)(2,1)} %param.8) | copy-start | bytes 442372
  31.1 13.0 %copy-start.4 = (bf16[128,128]{1,0:T(8,128)(2,1)S(1)}, bf16[128,128]{1,0:T(8,128)(2,1)}, u32[]{:S(2)}) copy-start(bf16[128,128]{1,0:T(8,128)(2,1)} %param.13) | copy-start | bytes 98308
  31.1 13.0 %copy-start.6 = (f32[128]{0:T(128)S(1)}, f32[128]{0:T(128)}, u32[]{:S(2)}) copy-start(f32[128]{0:T(128)} %param.11) | copy-start | bytes 1540
  40.5 11.7 %all-to-all-start.2 = ((bf16[8,96,96]{2,0,1:T(8,128)(2,1)}), bf16[8,96,96]{2,0,1:T(8,128)(2,1)S(1)}, u32[]{:S(2)}, u32[]{:S(2)}) async-start(bf16[8,96,96]{2,0,1:T(8,128)(2,1)} %copy.52), calls=%async_computation.2 | async-start | bytes 393216 | tf_op jit(solution)/shard_map/all_to_all | solution.py:50
  44.5 8.5 copy-start.2
  44.5 8.5 copy-start.3
  44.5 8.5 copy-start.5
  56.8 10.8 all-to-all-start.3
  68.8 10.6 all-to-all-start.5
  79.3 10.5 all-to-all-start.4
  82.9 1051.3 %all-reduce.4.cloned.1.call-start = ((), (), s32[]{:S(2)}) async-start(), calls=%async_computation.6 | async-start | bytes 786432 | tf_op jit(solution)/shard_map/psum | solution.py:105
Sparse Core Ops, SparseCore 0:
  263.8 870.3 all-reduce.3
where the time goes:
time: 1150 us
  waiting for transfers between devices  911 us (79%)
  blocking collectives  171 us (15%)
  starting transfers between devices  25.3 us (2%)
  between operations  15.1 us (1%)
    psum x1, waiting for transfers between devices, body(): lax.psum((proj_grad, gate_grad, out_weight_grad, in_gain_grad, out_gain_g...  869 us
    psum x1, blocking collectives, body(): lax.psum((proj_grad, gate_grad, out_weight_grad, in_gain_grad, out_gain_g...  171 us
  transfers between devices with their start and end apart: 7, of which 7 were waited for; matrix products, arithmetic and copies ran while one was open for 0% of the time, Pallas kernels for 0%

commit v1 on v0

--- a/solution.py
+++ b/solution.py
@@ -1,7 +1,10 @@
 import jax
 import jax.numpy as jnp
 from jax import lax
+from jax.sharding import Mesh
 from jax.sharding import PartitionSpec as P
+
+NEAR = ("zl", "core", "tile")
 
 
 def normalize(values, gain):
@@ -38,12 +41,10 @@
     gate_lin = jnp.dot(normed_in, gate_weight, preferred_element_type=jnp.float32)
     left_panel = (sig_left * lin_left * pair_mask).astype(jnp.bfloat16)
     right_panel = (sig_right * lin_right * pair_mask).astype(jnp.bfloat16)
-    left_flip = jnp.transpose(left_panel, (2, 0, 1))
-    right_flip = jnp.transpose(right_panel, (2, 0, 1))
-    left_chan, right_chan = (
-        lax.all_to_all(left_flip, "tile", split_axis=0, concat_axis=1, tiled=True),
-        lax.all_to_all(right_flip, "tile", split_axis=0, concat_axis=1, tiled=True),
-    )
+    both = jnp.concatenate([left_panel[..., None], right_panel[..., None]], axis=-1)
+    both_flip = jnp.transpose(both, (2, 3, 0, 1))
+    both_chan = lax.all_to_all(both_flip, "tile", split_axis=0, concat_axis=2, tiled=True)
+    left_chan, right_chan = both_chan[:, 0], both_chan[:, 1]
     tri_chan = jnp.einsum(
         "hik,hjk->hij", left_chan, right_chan, preferred_element_type=jnp.float32
     ).astype(jnp.bfloat16)
@@ -64,7 +65,6 @@
     )
     gate_grad = jnp.dot(flat_in.T, grad_gate.reshape(-1, chans), preferred_element_type=jnp.float32)
     grad_normed_out = jnp.dot(grad_update, out_weight.T, preferred_element_type=jnp.float32)
-    out_gain_grad = jnp.sum(grad_normed_out * scaled_out, axis=(0, 1))
     grad_tri = norm_back(grad_normed_out, scaled_out, inverse_out, out_gain).astype(jnp.bfloat16)
     grad_flip = jnp.transpose(grad_tri, (2, 0, 1))
     grad_chan = lax.all_to_all(grad_flip, "tile", split_axis=0, concat_axis=1, tiled=True)
@@ -75,12 +75,10 @@
     right_back = jnp.einsum(
         "hij,hik->hjk", grad_chan, left_again, preferred_element_type=jnp.float32
     ).astype(jnp.bfloat16)
-    left_rows, right_rows = (
-        lax.all_to_all(left_back, "tile", split_axis=1, concat_axis=0, tiled=True),
-        lax.all_to_all(right_back, "tile", split_axis=1, concat_axis=0, tiled=True),
-    )
-    left_grad = jnp.transpose(left_rows, (1, 2, 0)).astype(jnp.float32)
-    right_grad = jnp.transpose(right_rows, (1, 2, 0)).astype(jnp.float32)
+    back = jnp.stack([left_back, right_back], axis=1)
+    back_rows = lax.all_to_all(back, "tile", split_axis=2, concat_axis=0, tiled=True)
+    left_grad = jnp.transpose(back_rows[:, 0], (1, 2, 0)).astype(jnp.float32)
+    right_grad = jnp.transpose(back_rows[:, 1], (1, 2, 0)).astype(jnp.float32)
     grad_lin = jnp.concatenate(
         [
             (left_grad * sig_left * pair_mask).astype(jnp.bfloat16),
@@ -98,24 +96,48 @@
     grad_normed_in = jnp.dot(grad_lin, projections.T, preferred_element_type=jnp.float32) + jnp.dot(
         grad_gate, gate_weight.T, preferred_element_type=jnp.float32
     )
-    in_gain_grad = jnp.sum(grad_normed_in * scaled_in, axis=(0, 1))
     pair_grad = (upstream + norm_back(grad_normed_in, scaled_in, inverse_in, in_gain)).astype(
         jnp.bfloat16
     )
-    summed = lax.psum(
-        (proj_grad, gate_grad, out_weight_grad, in_gain_grad, out_gain_grad), ("grp", "tile")
-    )
-    return (pair_out[None], pair_grad[None], summed[0], summed[1], summed[2], summed[3], summed[4])
+    grads = reduce_grads(jnp.concatenate([proj_grad, gate_grad, out_weight_grad], axis=1))
+    proj_sum = grads[:, : 4 * width]
+    gate_sum = grads[:, 4 * width : 4 * width + chans]
+    out_sum = grads[:, 4 * width + chans :]
+    in_gain_grad = (
+        jnp.sum(proj_sum * projections.astype(jnp.float32), axis=1)
+        + jnp.sum(gate_sum * gate_weight.astype(jnp.float32), axis=1)
+    ) / in_gain
+    out_gain_grad = jnp.sum(out_sum * out_weight.astype(jnp.float32), axis=1) / out_gain
+    return (pair_out[None], pair_grad[None], proj_sum, gate_sum, out_sum, in_gain_grad, out_gain_grad)
+
+
+def exchange(pieces, axes):
+    return lax.all_to_all(pieces, axes, split_axis=0, concat_axis=0, tiled=True)
+
+
+def reduce_grads(grads):
+    near = lax.axis_size(NEAR)
+    far = lax.axis_size("zh")
+    rows, columns = grads.shape
+    pieces = grads.astype(jnp.bfloat16).reshape(near, rows // near, columns)
+    part = jnp.sum(exchange(pieces, NEAR).astype(jnp.float32), axis=0)
+    spread = jnp.broadcast_to(part.astype(jnp.bfloat16)[None], (far,) + part.shape)
+    whole = jnp.sum(exchange(spread, "zh").astype(jnp.float32), axis=0)
+    spread = jnp.broadcast_to(whole.astype(jnp.bfloat16)[None], (near,) + part.shape)
+    return exchange(spread, NEAR).astype(jnp.float32).reshape(rows, columns)
 
 
 def solution(mesh):
+    groups, tiles = mesh.devices.shape
+    mesh = Mesh(mesh.devices.reshape(groups // 4, 2, 2, tiles), ("zh",) + NEAR)
+    grp = ("zh", "zl", "core")
     return jax.shard_map(
         body,
         mesh=mesh,
         in_specs=(
-            P("grp", "tile", None, None),
-            P("grp", "tile", None, None),
-            P("grp"),
+            P(grp, "tile", None, None),
+            P(grp, "tile", None, None),
+            P(grp),
             P(),
             P(),
             P(),
@@ -123,8 +145,8 @@
             P(),
         ),
         out_specs=(
-            P("grp", "tile", None, None),
-            P("grp", "tile", None, None),
+            P(grp, "tile", None, None),
+            P(grp, "tile", None, None),
             P(),
             P(),
             P(),

time: 1150 us -> 150 us (0.13)
  waiting for transfers between devices: 911 us -> 14.4 us
  blocking collectives: 171 us -> 109 us
  starting transfers between devices: 25.3 us -> 7.07 us
  between operations: 15.1 us -> 1.68 us
    psum x1 -> x0, waiting for transfers between devices: 869 us -> none  [body(): lax.psum((proj_grad, gate_grad, out_weight_grad, in_gain_grad, out_gain_g...]
    psum x1 -> x0, blocking collectives: 171 us -> none  [body(): lax.psum((proj_grad, gate_grad, out_weight_grad, in_gain_grad, out_gain_g...]
    all_to_all x0 -> x5, blocking collectives: none -> 109 us  [the longest x3 82.5 us: exchange(): return lax.all_to_all(pieces, axes, split_axis=0, concat_axis=0, tiled=True)]
    all_to_all x5 -> x1, waiting for transfers between devices: 33.7 us -> 7.89 us  [body(): lax.all_to_all(back, 'tile', split_axis=2, concat_axis=0, tiled=True)]
    all_to_all x5 -> x1, starting transfers between devices: 21.8 us -> 3.55 us  [body(): lax.all_to_all(back, 'tile', split_axis=2, concat_axis=0, tiled=True)]
  transfers between devices with their start and end apart: 7 -> 2, of which waited for: 7 -> 2; matrix products, arithmetic and copies ran while one was open for 0% -> 1% of each run, Pallas kernels for 0% -> 0%
where the time goes in v1:
time: 150 us
  blocking collectives  109 us (73%)
  waiting for transfers between devices  14.4 us (10%)
  other arithmetic  7.62 us (5%)
  starting transfers between devices  7.07 us (5%)
  matrix products  5.64 us (4%)
  local copies, waits for them, and re-layouts  4.35 us (3%)
  between operations  1.68 us (1%)
    all_to_all x3, blocking collectives, exchange(): return lax.all_to_all(pieces, axes, split_axis=0, concat_axis=0, tiled=True)  82.5 us
    all_to_all x1, blocking collectives, body(): lax.all_to_all(both_flip, 'tile', split_axis=0, concat_axis=2, tiled=True)  15.4 us
    all_to_all x1, blocking collectives, body(): lax.all_to_all(grad_flip, 'tile', split_axis=0, concat_axis=1, tiled=True)  10.9 us
    all_to_all x1, waiting for transfers between devices, body(): lax.all_to_all(back, 'tile', split_axis=2, concat_axis=0, tiled=True)  7.89 us
    all_to_all x1, waiting for transfers between devices, body(): lax.all_to_all(tri_chan, 'tile', split_axis=1, concat_axis=0, tiled=True)  6.47 us
    all_to_all x1, starting transfers between devices, body(): lax.all_to_all(back, 'tile', split_axis=2, concat_axis=0, tiled=True)  3.55 us
    all_to_all x1, starting transfers between devices, body(): lax.all_to_all(tri_chan, 'tile', split_axis=1, concat_axis=0, tiled=True)  3.52 us
  transfers between devices with their start and end apart: 2, of which 2 were waited for; matrix products, arithmetic and copies ran while one was open for 1% of the time, Pallas kernels for 0%

profile of v1, /device:TPU:1, one launch (start us, length us, event | category | flops | bytes accessed | tf_op | source)
XLA Modules:
  0.0 149.5 jit_solution(15751165428971514486)
XLA Ops:
  0.6 1.1 convert_reduce_fusion
  1.7 1.2 fusion.21
  3.7 1.4 fusion.62
  5.1 0.2 fusion.55
  5.3 0.4 copy.114
  5.8 15.4 %all_to_all.78 = bf16[128,2,6,96]{3,1,2,0:T(2,128)(2,1)S(1)} all-to-all(bf16[128,2,6,96]{3,1,2,0:T(2,128)(2,1)S(1)} %copy.114), channel_id=1, replica_groups=mesh['zh'=16,'zl'=2,'core'=2,'tile'=16] {'tile'}, dimensions={0} | all-to-all | bytes 589824 | tf_op jit(solution)/shard_map/all_to_all | solution.py:46
  21.4 0.2 convolution_convert_fusion.2
  21.6 0.8 copy.119
  22.4 3.5 %all-to-all-start.1 = ((bf16[8,96,96]{2,0,1:T(8,128)(2,1)}), bf16[8,96,96]{2,0,1:T(8,128)(2,1)S(1)}, u32[]{:S(2)}, u32[]{:S(2)}) async-start(bf16[8,96,96]{2,0,1:T(8,128)(2,1)} %copy.119), calls=%async_computation.1 | async-start | bytes 393216 | tf_op jit(solution)/shard_map/all_to_all | solution.py:51
  25.9 0.3 fusion.3
  26.3 6.5 %all-to-all-done.1 = bf16[8,96,96]{2,0,1:T(8,128)(2,1)S(1)} async-done(((bf16[8,96,96]{2,0,1:T(8,128)(2,1)}), bf16[8,96,96]{2,0,1:T(8,128)(2,1)S(1)}, u32[]{:S(2)}, u32[]{:S(2)}) %all-to-all-start.1) | async-done | bytes 147488 | tf_op jit(solution)/shard_map/all_to_all | solution.py:51
  32.8 0.2 copy.121
  33.0 0.2 bitcast_reduce_fusion
  33.2 0.3 multiply_reduce_fusion.1
  33.5 0.5 fusion.77
  34.0 0.4 fusion.51
  34.4 0.2 copy.123
  34.6 10.9 %all_to_all.79 = bf16[128,6,96]{2,1,0:T(8,128)(2,1)S(1)} all-to-all(bf16[128,6,96]{2,1,0:T(8,128)(2,1)S(1)} %copy.123), channel_id=1, replica_groups=mesh['zh'=16,'zl'=2,'core'=2,'tile'=16] {'tile'}, dimensions={0} | all-to-all | bytes 294912 | tf_op jit(solution)/shard_map/all_to_all | solution.py:70
  45.5 0.2 copy.127
  45.7 0.3 fusion.4
  46.0 0.2 fusion.5
  46.2 0.1 pad_maximum_fusion.1
  46.3 0.9 copy.128
  47.2 3.6 %all-to-all-start.3 = ((bf16[8,2,96,96]{3,0,1,2:T(8,128)(2,1)}), bf16[8,2,96,96]{3,0,1,2:T(8,128)(2,1)S(1)}, u32[]{:S(2)}, u32[]{:S(2)}) async-start(bf16[8,2,96,96]{3,0,1,2:T(8,128)(2,1)} %copy.128), calls=%async_computation.3 | async-start | bytes 786432 | tf_op jit(solution)/shard_map/all_to_all | solution.py:79
  50.7 0.4 fusion.8
  51.2 1.0 fusion.26
  52.2 7.9 %all-to-all-done.3 = bf16[8,2,96,96]{3,0,1,2:T(8,128)(2,1)S(1)} async-done(((bf16[8,2,96,96]{3,0,1,2:T(8,128)(2,1)}), bf16[8,2,96,96]{3,0,1,2:T(8,128)(2,1)S(1)}, u32[]{:S(2)}, u32[]{:S(2)}) %all-to-all-start.3) | async-done | bytes 294944 | tf_op jit(solution)/shard_map/all_to_all | solution.py:79
  60.1 0.1 copy.161
  60.2 0.2 copy.146
  60.4 0.2 copy.147
  60.5 0.3 fusion.45
  60.9 0.4 copy-done.2
  61.3 0.3 fusion.60
  61.6 0.5 fusion.76
  62.1 1.0 fusion.64
  63.1 0.2 copy.133
  63.3 0.3 fusion.6
  63.6 0.2 fusion.7
  63.9 0.2 copy.137
  64.1 27.4 %all_to_all.80 = bf16[64,2,768]{2,1,0:T(2,128)(2,1)S(1)} all-to-all(bf16[64,2,768]{2,1,0:T(2,128)(2,1)S(1)} %copy.137), channel_id=1, replica_groups=mesh['zh'=16,'zl'=2,'core'=2,'tile'=16] {'zl','core','tile'}, dimensions={0} | all-to-all | bytes 393216 | tf_op jit(solution)/shard_map/all_to_all | solution.py:115
  91.5 0.2 reduce_sum.131
  91.8 40.3 %all_to_all.81 = bf16[16,2,768]{2,1,0:T(2,128)(2,1)S(1)} all-to-all(bf16[16,2,768]{2,1,0:T(2,128)(2,1)S(1)} %broadcast_in_dim.16), channel_id=1, replica_groups=mesh['zh'=16,'zl'=2,'core'=2,'tile'=16] {'zh'}, dimensions={0} | all-to-all | bytes 98304 | tf_op jit(solution)/shard_map/all_to_all | solution.py:115
  132.1 0.1 broadcast_in_dim.17
  132.2 14.8 %all_to_all.82 = bf16[64,2,768]{2,1,0:T(2,128)(2,1)S(1)} all-to-all(bf16[64,2,768]{2,1,0:T(2,128)(2,1)S(1)} %broadcast_in_dim.17), channel_id=1, replica_groups=mesh['zh'=16,'zl'=2,'core'=2,'tile'=16] {'zl','core','tile'}, dimensions={0} | all-to-all | bytes 393216 | tf_op jit(solution)/shard_map/all_to_all | solution.py:115
  147.1 0.7 multiply_reduce_fusion.2
  147.8 0.7 multiply_reduce_fusion.3
  148.5 0.5 div.51
  149.0 0.5 add_divide_fusion
  (35 shorter events, 0.7 us)
Async XLA Ops:
  21.3 4.6 %copy-start = (bf16[1,6,96,128]{3,2,1,0:T(8,128)(2,1)S(1)}, bf16[1,6,96,128]{3,2,1,0:T(8,128)(2,1)}, u32[]{:S(2)}) copy-start(bf16[1,6,96,128]{3,2,1,0:T(8,128)(2,1)} %param.8) | copy-start | bytes 442372
  21.3 4.6 %copy-start.4 = (bf16[128,128]{1,0:T(8,128)(2,1)S(1)}, bf16[128,128]{1,0:T(8,128)(2,1)}, u32[]{:S(2)}) copy-start(bf16[128,128]{1,0:T(8,128)(2,1)} %param.13) | copy-start | bytes 98308
  21.3 4.6 %copy-start.5 = (f32[128]{0:T(128)S(1)}, f32[128]{0:T(128)}, u32[]{:S(2)}) copy-start(f32[128]{0:T(128)} %param.11) | copy-start | bytes 1540
  22.4 10.4 %all-to-all-start.1 = ((bf16[8,96,96]{2,0,1:T(8,128)(2,1)}), bf16[8,96,96]{2,0,1:T(8,128)(2,1)S(1)}, u32[]{:S(2)}, u32[]{:S(2)}) async-start(bf16[8,96,96]{2,0,1:T(8,128)(2,1)} %copy.119), calls=%async_computation.1 | async-start | bytes 393216 | tf_op jit(solution)/shard_map/all_to_all | solution.py:51
  26.3 7.2 %copy-start.1 = (bf16[1,6,96,128]{3,2,1,0:T(8,128)(2,1)S(1)}, bf16[1,6,96,128]{3,2,1,0:T(8,128)(2,1)}, u32[]{:S(2)}) copy-start(bf16[1,6,96,128]{3,2,1,0:T(8,128)(2,1)} %param.9) | copy-start | bytes 442372
  26.3 7.2 %copy-start.3 = (bf16[128,128]{1,0:T(8,128)(2,1)S(1)}, bf16[128,128]{1,0:T(8,128)(2,1)}, u32[]{:S(2)}) copy-start(bf16[128,128]{1,0:T(8,128)(2,1)} %param.15) | copy-start | bytes 98308
  26.3 7.2 %copy-start.6 = (f32[128]{0:T(128)S(1)}, f32[128]{0:T(128)}, u32[]{:S(2)}) copy-start(f32[128]{0:T(128)} %param.14) | copy-start | bytes 1540
  47.2 12.9 %all-to-all-start.3 = ((bf16[8,2,96,96]{3,0,1,2:T(8,128)(2,1)}), bf16[8,2,96,96]{3,0,1,2:T(8,128)(2,1)S(1)}, u32[]{:S(2)}, u32[]{:S(2)}) async-start(bf16[8,2,96,96]{3,0,1,2:T(8,128)(2,1)} %copy.128), calls=%async_computation.3 | async-start | bytes 786432 | tf_op jit(solution)/shard_map/all_to_all | solution.py:79
  60.4 0.9 copy-start.2

commit v2 on v0

v2 whole, which is shorter than its diff:
```python
import functools

import jax
import jax.numpy as jnp
from jax import lax
from jax.experimental import pallas as pl
from jax.experimental.pallas import tpu as pltpu
from jax.sharding import Mesh
from jax.sharding import PartitionSpec as P

NEAR = ("zl", "core", "tile")
LANES = 128
EPS = 1e-05
F32 = jnp.float32
BF16 = jnp.bfloat16


def mat(a, b):
    return jnp.dot(a, b, preferred_element_type=F32)


def mat_nt(a, b):
    return lax.dot_general(a, b, (((1,), (1,)), ((), ())), preferred_element_type=F32)


def flip(values):
    return values.astype(F32).T.astype(values.dtype)


def pad_rows(values, rows):
    return jnp.concatenate(
        [values, jnp.zeros((rows - values.shape[0], values.shape[1]), values.dtype)], axis=0
    )


def row_norm(values):
    centred = values - jnp.mean(values, axis=1, keepdims=True)
    inverse = lax.rsqrt(jnp.mean(centred * centred, axis=1, keepdims=True) + EPS)
    return centred * inverse, inverse


def normed_row(rep_ref, gain, i):
    scaled, _ = row_norm(rep_ref[i].astype(F32))
    return pad_rows((scaled * gain).astype(BF16), LANES)


def masks(info_ref, i):
    length = info_ref[0]
    lane = lax.broadcasted_iota(jnp.int32, (1, LANES), 1)
    inside = jnp.logical_and(lane < length, info_ref[1] + i < length)
    return inside.astype(F32)


def gated(linear, width):
    return (
        linear[:width],
        jax.nn.sigmoid(linear[width : 2 * width]),
        linear[2 * width : 3 * width],
        jax.nn.sigmoid(linear[3 * width :]),
    )


def put_panel(out_ref, start, pair, first, second):
    peers = out_ref.shape[0]
    first = first.reshape(peers, -1, LANES)
    second = second.reshape(peers, -1, LANES)
    both = jnp.concatenate([first, second], axis=1).astype(BF16)
    size = both.shape[1]
    out_ref[:, start + pair * size : start + (pair + 1) * size, :] = both


def get_panel(in_ref, start, pair, size):
    both = in_ref[:, start + pair * size : start + (pair + 1) * size, :].astype(F32)
    half = size // 2
    return both[:, :half].reshape(-1, LANES), both[:, half:].reshape(-1, LANES)


def panels_kernel(info_ref, rep_ref, gain_ref, proj_ref, out_ref):
    rows = rep_ref.shape[0]
    width = proj_ref.shape[1] // 4
    half = out_ref.shape[1] // 2
    proj = flip(proj_ref[...])
    gain = gain_ref[...]
    for pair in range(rows // 2):
        left, right = [], []
        for i in (2 * pair, 2 * pair + 1):
            linear = mat_nt(proj, normed_row(rep_ref, gain, i))
            lin_left, sig_left, lin_right, sig_right = gated(linear, width)
            mask = masks(info_ref, i)
            left.append(sig_left * lin_left * mask)
            right.append(sig_right * lin_right * mask)
        put_panel(out_ref, 0, pair, *left)
        put_panel(out_ref, half, pair, *right)


def early_kernel(
    info_ref, rep_ref, cot_ref, gain_ref, proj_ref, gate_ref, out_gain_ref, out_weight_ref,
    normed_ref, factor_ref, sig_ref, update_ref, slope_ref, upstream_ref,
):
    rows, _, chans = rep_ref.shape
    width = proj_ref.shape[1] // 4
    proj = flip(proj_ref[...])
    gate = flip(gate_ref[...])
    out_weight = out_weight_ref[...]
    gain = gain_ref[...]
    out_gain = jnp.broadcast_to(out_gain_ref[...], (LANES, width)).T
    for i in range(rows):
        normed = normed_row(rep_ref, gain, i)
        normed_ref[i] = normed
        lin_left, sig_left, lin_right, sig_right = gated(mat_nt(proj, normed), width)
        mask = masks(info_ref, i)
        factor_ref[i, :width] = sig_left * mask
        factor_ref[i, width : 2 * width] = lin_left * mask * sig_left * (1.0 - sig_left)
        factor_ref[i, 2 * width : 3 * width] = sig_right * mask
        factor_ref[i, 3 * width :] = lin_right * mask * sig_right * (1.0 - sig_right)
        sig = jax.nn.sigmoid(mat_nt(gate, normed))
        cot = pad_rows(cot_ref[i].astype(F32), LANES).T
        update = (sig * cot).astype(BF16)
        sig_ref[i] = sig
        slope_ref[i] = cot * sig * (1.0 - sig)
        update_ref[i] = update
        upstream_ref[i] = mat(out_weight, update) * out_gain


def spread_rows(ref, scratch):
    scratch[...] = ref.astype(F32).reshape(scratch.shape)


def triangle_kernel(panel_ref, out_ref, left_ref, right_ref, tri_ref):
    peers, both, _ = panel_ref.shape
    half = both // 2
    total = out_ref.shape[0] * out_ref.shape[1]
    chans = LANES // peers
    residues = total // chans
    spread_rows(panel_ref[:, :half, :], left_ref)
    spread_rows(panel_ref[:, half:, :], right_ref)
    for h in range(chans):
        rows = pl.ds(h, residues, stride=chans)
        left = left_ref[rows, :].astype(BF16)
        right = pad_rows(right_ref[rows, :].astype(BF16), LANES)
        tri_ref[rows, :] = mat_nt(left, right)
    out_ref[...] = tri_ref[...].astype(BF16).reshape(out_ref.shape)


def out_norm(triangle):
    centred = triangle - jnp.mean(triangle, axis=0, keepdims=True)
    inverse = lax.rsqrt(jnp.mean(centred * centred, axis=0, keepdims=True) + EPS)
    return centred * inverse, inverse


def grad_tri_kernel(tri_ref, upstream_ref, out_ref):
    rows = upstream_ref.shape[0]
    size = out_ref.shape[1] // (rows // 2)
    for pair in range(rows // 2):
        grads = []
        for i, triangle in zip((2 * pair, 2 * pair + 1), get_panel(tri_ref, 0, pair, size)):
            scaled, inverse = out_norm(triangle)
            grad = upstream_ref[i]
            first_mean = jnp.mean(grad, axis=0, keepdims=True)
            second_mean = jnp.mean(grad * scaled, axis=0, keepdims=True)
            grads.append(inverse * (grad - first_mean - scaled * second_mean))
        put_panel(out_ref, 0, pair, *grads)


def update_kernel(
    rep_ref, tri_ref, normed_ref, sig_ref, update_ref, slope_ref, out_gain_ref, out_weight_ref,
    pair_out_ref, grad_gate_ref, grads_ref,
):
    rows, residues, chans = rep_ref.shape
    width = out_weight_ref.shape[0]
    out_weight = flip(out_weight_ref[...])
    out_gain = jnp.broadcast_to(out_gain_ref[...], (LANES, width)).T
    size = tri_ref.shape[1] // (rows // 2)
    gate_sum = jnp.zeros((chans, chans), F32)
    out_sum = jnp.zeros((chans, width), F32)
    for pair in range(rows // 2):
        for i, triangle in zip((2 * pair, 2 * pair + 1), get_panel(tri_ref, 0, pair, size)):
            scaled, _ = out_norm(triangle)
            normed_out = (scaled * out_gain).astype(BF16)
            update = mat(out_weight, normed_out)
            change = (sig_ref[i] * update).T
            pair_out_ref[i] = (rep_ref[i].astype(F32) + change[:residues]).astype(BF16)
            grad_gate = (slope_ref[i] * update).astype(BF16)
            grad_gate_ref[i] = grad_gate
            gate_sum += mat(grad_gate, normed_ref[i])
            out_sum += mat_nt(update_ref[i], normed_out)
    grads_ref[:chans] = gate_sum
    grads_ref[chans:] = out_sum


def back_kernel(panel_ref, grad_ref, out_ref, left_ref, right_ref, tri_ref, left_out, right_out):
    peers, both, _ = panel_ref.shape
    half = both // 2
    chans = LANES // peers
    residues = left_ref.shape[0] // chans
    spread_rows(panel_ref[:, :half, :], left_ref)
    spread_rows(panel_ref[:, half:, :], right_ref)
    spread_rows(grad_ref[...], tri_ref)
    for h in range(chans):
        rows = pl.ds(h, residues, stride=chans)
        left = left_ref[rows, :].astype(BF16)
        right = pad_rows(right_ref[rows, :].astype(BF16), LANES)
        grad = tri_ref[rows, :]
        left_out[rows, :] = mat(grad.astype(BF16), right)
        turned = pad_rows(grad, LANES).T.astype(BF16)
        right_out[rows, :] = mat(turned, pad_rows(left, LANES))[:residues]
    shape = (peers, half, LANES)
    out_ref[:, :half, :] = left_out[...].astype(BF16).reshape(shape)
    out_ref[:, half:, :] = right_out[...].astype(BF16).reshape(shape)


def proj_grad_kernel(back_ref, factor_ref, normed_ref, grads_ref, lin_ref, out_ref, rows_ref):
    rows, wide, _ = factor_ref.shape
    half = back_ref.shape[1] // 2
    size = half // (rows // 2)
    width = wide // 4
    near, piece, _ = out_ref.shape
    proj_sum = jnp.zeros((wide, normed_ref.shape[2]), F32)
    for pair in range(rows // 2):
        lefts = get_panel(back_ref, 0, pair, size)
        rights = get_panel(back_ref, half, pair, size)
        for i, left, right in zip((2 * pair, 2 * pair + 1), lefts, rights):
            lin = jnp.concatenate(
                [
                    (left * factor_ref[i, :width]).astype(BF16),
                    (left * factor_ref[i, width : 2 * width]).astype(BF16),
                    (right * factor_ref[i, 2 * width : 3 * width]).astype(BF16),
                    (right * factor_ref[i, 3 * width :]).astype(BF16),
                ],
                axis=0,
            )
            lin_ref[i] = lin
            proj_sum += mat(lin, normed_ref[i])
    main = wide // near
    extra = grads_ref.shape[0] // near
    rows_ref[...] = jnp.zeros(rows_ref.shape, F32)
    for s in range(main):
        rows_ref[pl.ds(s, near, stride=piece), :] = proj_sum[s * near : (s + 1) * near]
    for s in range(extra):
        rows_ref[pl.ds(main + s, near, stride=piece), :] = grads_ref[s * near : (s + 1) * near]
    out_ref[...] = rows_ref[...].astype(BF16).reshape(out_ref.shape)


def pair_grad_kernel(
    rep_ref, cot_ref, lin_ref, grad_gate_ref, gain_ref, proj_ref, gate_ref, out_ref
):
    rows, residues, _ = rep_ref.shape
    proj = proj_ref[...]
    gate = gate_ref[...]
    gain = gain_ref[...]
    for i in range(rows):
        grad = (mat(proj, lin_ref[i]) + mat(gate, grad_gate_ref[i])).T[:residues] * gain
        scaled, inverse = row_norm(rep_ref[i].astype(F32))
        first_mean = jnp.mean(grad, axis=1, keepdims=True)
        second_mean = jnp.mean(grad * scaled, axis=1, keepdims=True)
        change = inverse * (grad - first_mean - scaled * second_mean)
        out_ref[i] = (cot_ref[i].astype(F32) + change).astype(BF16)


def final_kernel(
    sum_ref, proj_ref, gate_ref, out_weight_ref, gain_ref, out_gain_ref,
    proj_grad_ref, gate_grad_ref, out_grad_ref, gain_grad_ref, out_gain_grad_ref, rows_ref,
):
    near, piece, _ = sum_ref.shape
    chans, wide = proj_ref.shape
    main = wide // near
    extra = (chans + out_weight_ref.shape[0]) // near
    rows_ref[...] = sum_ref[...].astype(F32).reshape(rows_ref.shape)
    take = lambda s: rows_ref[pl.ds(s, near, stride=piece), :]
    proj_sum = jnp.concatenate([take(s) for s in range(main)], axis=0)
    rest = jnp.concatenate([take(main + s) for s in range(extra)], axis=0)
    proj_sum = proj_sum.T
    gate_sum = rest[:chans].T
    out_sum = rest[chans:].T
    proj_grad_ref[...] = proj_sum
    gate_grad_ref[...] = gate_sum
    out_grad_ref[...] = out_sum
    gains = jnp.sum(proj_sum * proj_ref[...].astype(F32), axis=1, keepdims=True) + jnp.sum(
        gate_sum * gate_ref[...].astype(F32), axis=1, keepdims=True
    )
    outs = jnp.sum(out_sum * out_weight_ref[...].astype(F32), axis=1, keepdims=True)
    gain_grad_ref[...] = jnp.broadcast_to(gains, (chans, LANES)).T[:1] / gain_ref[...]
    out_gain_grad_ref[...] = jnp.broadcast_to(outs, (chans, LANES)).T[:1] / out_gain_ref[...]


def call(kernel, outs, *args, smem=0, scratch=(), flops=0):
    vmem = pl.BlockSpec(memory_space=pltpu.VMEM)
    size = sum(a.size * a.dtype.itemsize for a in args)
    shapes = [jax.ShapeDtypeStruct(shape, dtype) for shape, dtype in outs]
    return pl.pallas_call(
        kernel,
        out_shape=shapes,
        in_specs=[pl.BlockSpec(memory_space=pltpu.SMEM)] * smem + [vmem] * (len(args) - smem),
        out_specs=[vmem] * len(shapes),
        scratch_shapes=[pltpu.VMEM(shape, F32) for shape in scratch],
        compiler_params=pltpu.CompilerParams(vmem_limit_bytes=32 * 1024 * 1024),
        cost_estimate=pl.CostEstimate(flops=flops, bytes_accessed=size, transcendentals=0),
    )(*args)


def exchange(pieces, axes):
    return lax.all_to_all(pieces, axes, split_axis=0, concat_axis=0, tiled=True)


def total(pieces):
    return jnp.sum(pieces.astype(F32), axis=0).astype(BF16)


def spread(part, count):
    return jnp.broadcast_to(part[None], (count,) + part.shape)


def body(pair_rep, cotangent, lengths, in_gain, projections, gate_weight, out_gain, out_weight):
    tiles = lax.axis_size("tile")
    near = lax.axis_size(NEAR)
    far = lax.axis_size("zh")
    rep, cot = pair_rep[0], cotangent[0]
    rows, residues, chans = rep.shape
    wide = projections.shape[1]
    width = wide // 4
    panel = rows * width // tiles
    lines = residues * width // tiles
    info = jnp.stack([lengths[0], lax.axis_index("tile") * rows])
    gain, gain_o = in_gain[None], out_gain[None]
    grid = (rows, LANES, LANES)

    (panels,) = call(
        panels_kernel, [((tiles, 2 * panel, LANES), BF16)], info, rep, gain, projections, smem=1
    )
    sides = exchange(panels, "tile")
    normed, factor, sig, update, slope, upstream = call(
        early_kernel,
        [
            (grid, BF16), ((rows, wide, LANES), F32), (grid, F32), (grid, BF16), (grid, F32),
            (grid, F32),
        ],
        info, rep, cot, gain, projections, gate_weight, gain_o, out_weight, smem=1,
        flops=10**9,
    )
    (tri_chan,) = call(
        triangle_kernel, [((tiles, panel, LANES), BF16)], sides, scratch=[(lines, LANES)] * 3
    )
    tri_rows = exchange(tri_chan, "tile")
    (grad_rows,) = call(
        grad_tri_kernel, [((tiles, panel, LANES), BF16)], tri_rows, upstream
    )
    grad_chan = exchange(grad_rows, "tile")
    pair_out, grad_gate, grads = call(
        update_kernel,
        [(rep.shape, BF16), (grid, BF16), ((2 * chans, width), F32)],
        rep, tri_rows, normed, sig, update, slope, gain_o, out_weight, flops=10**9,
    )
    (back,) = call(
        back_kernel, [((tiles, 2 * panel, LANES), BF16)], sides, grad_chan,
        scratch=[(lines, LANES)] * 5,
    )
    back_rows = exchange(back, "tile")
    piece = -(-(wide + 2 * chans) // near // 16) * 16
    lin, pieces = call(
        proj_grad_kernel, [((rows, wide, LANES), BF16), ((near, piece, LANES), BF16)],
        back_rows, factor, normed, grads, scratch=[(near * piece, LANES)],
    )
    part = total(exchange(pieces, NEAR))
    (pair_grad,) = call(
        pair_grad_kernel, [(rep.shape, BF16)], rep, cot, lin, grad_gate, gain, projections,
        gate_weight, flops=10**9,
    )
    whole = total(exchange(spread(part, far), "zh"))
    sums = exchange(spread(whole, near), NEAR)
    proj_grad, gate_grad, out_grad, gain_grad, gain_o_grad = call(
        final_kernel,
        [
            ((chans, wide), F32), ((chans, chans), F32), ((width, chans), F32),
            ((1, chans), F32), ((1, width), F32),
        ],
        sums, projections, gate_weight, out_weight, gain, gain_o,
        scratch=[(near * piece, LANES)],
    )
    return (
        pair_out[None], pair_grad[None], proj_grad, gate_grad, out_grad,
        gain_grad[0], gain_o_grad[0],
    )


def solution(mesh):
    groups, tiles = mesh.devices.shape
    close = 4 if groups % 4 == 0 else 1
    devices = mesh.devices.reshape(groups // close, max(close // 2, 1), min(close, 2), tiles)
    mesh = Mesh(devices, ("zh",) + NEAR)
    grp = ("zh", "zl", "core")
    rows = P(grp, "tile", None, None)
    return jax.shard_map(
        body,
        mesh=mesh,
        in_specs=(rows, rows, P(grp), P(), P(), P(), P(), P()),
        out_specs=(rows, rows, P(), P(), P(), P(), P()),
        check_vma=False,
    )
```

time: 1150 us -> 146 us (0.13)
  waiting for transfers between devices: 911 us -> 16.9 us
  blocking collectives: 171 us -> 94.2 us
  between operations: 15.1 us -> 1.49 us
    psum x1 -> x0, waiting for transfers between devices: 869 us -> none  [body(): lax.psum((proj_grad, gate_grad, out_weight_grad, in_gain_grad, out_gain_g...]
    psum x1 -> x0, blocking collectives: 171 us -> none  [body(): lax.psum((proj_grad, gate_grad, out_weight_grad, in_gain_grad, out_gain_g...]
    all_to_all x0 -> x4, blocking collectives: none -> 94.2 us  [exchange(): return lax.all_to_all(pieces, axes, split_axis=0, concat_axis=0, tiled=True)]
    all_to_all x6 -> x3, waiting for transfers between devices: 41.4 us -> 16.9 us  [exchange(): return lax.all_to_all(pieces, axes, split_axis=0, concat_axis=0, tiled=True)]
    all_to_all x6 -> x3, starting transfers between devices: 25.3 us -> 14.9 us  [exchange(): return lax.all_to_all(pieces, axes, split_axis=0, concat_axis=0, tiled=True)]
  transfers between devices with their start and end apart: 7 -> 3, of which waited for: 7 -> 3; matrix products, arithmetic and copies ran while one was open for 0% -> 0% of each run, Pallas kernels for 0% -> 3%
where the time goes in v2:
time: 146 us; the launch traced here: 145 us
  blocking collectives  94.2 us (65%)
  waiting for transfers between devices  16.9 us (12%)
  starting transfers between devices  14.9 us (10%)
  Pallas kernels  10.1 us (7%)
  local copies, waits for them, and re-layouts  7.6 us (5%)
  between operations  1.49 us (1%)
    all_to_all x4, blocking collectives, exchange(): return lax.all_to_all(pieces, axes, split_axis=0, concat_axis=0, tiled=True)  94.2 us
    all_to_all x3, waiting for transfers between devices, exchange(): return lax.all_to_all(pieces, axes, split_axis=0, concat_axis=0, tiled=True)  16.9 us
    all_to_all x3, starting transfers between devices, exchange(): return lax.all_to_all(pieces, axes, split_axis=0, concat_axis=0, tiled=True)  14.9 us
    pallas_call x9, Pallas kernels, call(): pl.pallas_call(kernel, out_shape=shapes, in_specs=[pl.BlockSpec(memory_sp...  10.1 us
    unnamed x32, local copies, waits for them, and re-layouts  6.85 us
  transfers between devices with their start and end apart: 3, of which 3 were waited for; matrix products, arithmetic and copies ran while one was open for 0% of the time, Pallas kernels for 3%

profile of v2, /device:TPU:1, one launch (start us, length us, event | category | flops | bytes accessed | tf_op | source)
XLA Modules:
  0.0 145.5 jit_solution(116357723474104181)
XLA Ops:
  0.6 0.0 copy-start.7
  0.6 0.0 copy-start.8
  1.3 0.1 pad_add_fusion.info_ref
  1.4 0.0 copy-start
  1.4 0.9 copy-done
  2.3 0.0 copy-start.2
  2.3 0.9 copy-done.2
  3.2 0.0 copy-start.6
  3.2 0.7 copy-done.6
  3.9 0.0 copy-start.1
  3.9 0.0 copy-start.11
  3.9 1.2 shard_map.135
  5.1 15.4 %all_to_all.35.panel_ref = bf16[16,96,128]{2,1,0:T(8,128)(2,1)S(1)} all-to-all(bf16[16,96,128]{2,1,0:T(8,128)(2,1)S(1)} %shard_map.135), channel_id=1, replica_groups=mesh['zh'=16,'zl'=2,'core'=2,'tile'=16] {'tile'}, dimensions={0} | all-to-all | bytes 786432 | tf_op jit(solution)/shard_map/all_to_all | solution.py:302
  20.5 1.0 shard_map.136
  21.4 3.5 %all-to-all-start.1 = ((bf16[16,48,128]{2,1,0:T(8,128)(2,1)}), bf16[16,48,128]{2,1,0:T(8,128)(2,1)S(1)}, u32[]{:S(2)}, u32[]{:S(2)}) async-start(bf16[16,48,128]{2,1,0:T(8,128)(2,1)} %shard_map.136), calls=%async_computation.1 | async-start | bytes 393216 | tf_op jit(solution)/shard_map/all_to_all | solution.py:302
  25.0 0.0 copy-done.7
  25.0 0.0 copy-done.8
  25.0 0.0 copy-done.1
  25.0 0.0 copy-done.3
  25.0 0.0 copy-done.4
  25.0 0.0 copy-done.5
  25.0 0.0 copy-done.11
  25.0 1.8 %shard_map.137 = (bf16[6,128,128]{2,1,0:T(8,128)(2,1)S(1)}, f32[6,512,128]{2,1,0:T(8,128)S(1)}, f32[6,128,128]{2,1,0:T(8,128)S(1)}, bf16[6,128,128]{2,1,0:T(8,12...) custom-call(s32[2]{0:T(128)S(1)} %pad_add_fusion.info_ref, bf16[6,96,128]{2,1,0:T(8,128)(2,1)S(1)} %bitcast.10, ...), custom_call_target="tpu_custom_call" | custom-call | flops 1000000000 | bytes 492552 | tf_op jit(solution)/shard_map/pallas_call | solution.py:290
  26.8 0.0 copy-start.12
  26.8 0.7 copy-done.12
  27.6 0.7 copy-done.14
  28.3 3.6 %all-to-all-done.1.tri_ref = bf16[16,48,128]{2,1,0:T(8,128)(2,1)S(1)} async-done(((bf16[16,48,128]{2,1,0:T(8,128)(2,1)}), bf16[16,48,128]{2,1,0:T(8,128)(2,1)S(1)}, u32[]{:S(2)}, u32[]{:S(2)}) %all-to-all-start.1) | async-done | bytes 196640 | tf_op jit(solution)/shard_map/all_to_all | solution.py:302
  32.0 0.2 shard_map.139
  32.2 10.1 %all_to_all.36.grad_ref = bf16[16,48,128]{2,1,0:T(8,128)(2,1)S(1)} all-to-all(bf16[16,48,128]{2,1,0:T(8,128)(2,1)S(1)} %shard_map.139), channel_id=1, replica_groups=mesh['zh'=16,'zl'=2,'core'=2,'tile'=16] {'tile'}, dimensions={0} | all-to-all | bytes 393216 | tf_op jit(solution)/shard_map/all_to_all | solution.py:302
  42.3 1.2 shard_map.140
  43.6 3.9 %all-to-all-start.3 = ((bf16[16,96,128]{2,1,0:T(8,128)(2,1)}), bf16[16,96,128]{2,1,0:T(8,128)(2,1)S(1)}, u32[]{:S(2)}, u32[]{:S(2)}) async-start(bf16[16,96,128]{2,1,0:T(8,128)(2,1)} %shard_map.140), calls=%async_computation.3 | async-start | bytes 786432 | tf_op jit(solution)/shard_map/all_to_all | solution.py:302
  47.5 0.0 copy-start.13
  47.5 1.0 copy-done.13
  48.5 1.0 copy-done.15
  49.5 1.6 %shard_map.138 = (bf16[6,96,128]{2,1,0:T(8,128)(2,1)}, bf16[6,128,128]{2,1,0:T(8,128)(2,1)S(1)}, f32[256,128]{1,0:T(8,128)S(1)}) custom-call(bf16[6,96,128]{2,1,0:T(8,128)(2,1)S(1)} %bitcast.11, bf16[16,48,128]{2,1,0:T(8,128)(2,1)S(1)} %all-to-all-done.1.tri_ref, bf16[6,128,128]{2,1,0:T(8,128)(2,1)S(1)} %get-tuple-element.23.normed_ref, ...), custom_call_target="tpu_custom_call" | custom-call | flops 1000000000 | bytes 1556992 | tf_op jit(solution)/shard_map/pallas_call | solution.py:290
  51.1 5.7 %all-to-all-done.3.back_ref = bf16[16,96,128]{2,1,0:T(8,128)(2,1)S(1)} async-done(((bf16[16,96,128]{2,1,0:T(8,128)(2,1)}), bf16[16,96,128]{2,1,0:T(8,128)(2,1)S(1)}, u32[]{:S(2)}, u32[]{:S(2)}) %all-to-all-start.3) | async-done | bytes 393248 | tf_op jit(solution)/shard_map/all_to_all | solution.py:302
  56.8 0.5 shard_map.141
  57.3 0.0 copy-start.9
  57.3 0.9 copy-done.9
  58.1 27.9 %all_to_all.37 = bf16[64,16,128]{2,1,0:T(8,128)(2,1)S(1)} all-to-all(bf16[64,16,128]{2,1,0:T(8,128)(2,1)S(1)} %get-tuple-element.33), channel_id=1, replica_groups=mesh['zh'=16,'zl'=2,'core'=2,'tile'=16] {'zl','core','tile'}, dimensions={0} | all-to-all | bytes 524288 | tf_op jit(solution)/shard_map/all_to_all | solution.py:302
  86.0 0.1 reduce_sum.24
  86.1 40.9 %all_to_all.38 = bf16[16,16,128]{2,1,0:T(8,128)(2,1)S(1)} all-to-all(bf16[16,16,128]{2,1,0:T(8,128)(2,1)S(1)} %broadcast_in_dim.28), channel_id=1, replica_groups=mesh['zh'=16,'zl'=2,'core'=2,'tile'=16] {'zh'}, dimensions={0} | all-to-all | bytes 131072 | tf_op jit(solution)/shard_map/all_to_all | solution.py:302
  127.0 0.7 broadcast_in_dim.29
  127.7 7.5 %all-to-all-start.6 = ((bf16[64,16,128]{2,1,0:T(8,128)(2,1)}), bf16[64,16,128]{2,1,0:T(8,128)(2,1)S(1)}, u32[]{:S(2)}, u32[]{:S(2)}) async-start(bf16[64,16,128]{2,1,0:T(8,128)(2,1)} %broadcast_in_dim.29), calls=%async_computation.6 | async-start | bytes 524288 | tf_op jit(solution)/shard_map/all_to_all | solution.py:302
  135.2 0.0 copy-done.10
  135.2 1.7 %shard_map.142 = bf16[6,96,128]{2,1,0:T(8,128)(2,1)} custom-call(bf16[6,96,128]{2,1,0:T(8,128)(2,1)S(1)} %bitcast.12, bf16[6,96,128]{2,1,0:T(8,128)(2,1)S(1)} %bitcast.21, bf16[6,512,128]{2,1,0:T(8,128)(2,1)S(1)} %copy-done.10, bf16[6,128,128]{2,1,0:T(8,128)(2,1)S(1)} %get-tuple-element.32.grad_gate_ref, f32[1,128]{1,0:T(1,128)S(1)} %bitcast.15, ...), custom_call_target="tpu_custom_call" | custom-call | flops 1000000000 | bytes 1442304 | tf_op jit(solution)/shard_map/pallas_call | solution.py:290
  136.9 7.6 %all-to-all-done.6.sum_ref = bf16[64,16,128]{2,1,0:T(8,128)(2,1)S(1)} async-done(((bf16[64,16,128]{2,1,0:T(8,128)(2,1)}), bf16[64,16,128]{2,1,0:T(8,128)(2,1)S(1)}, u32[]{:S(2)}, u32[]{:S(2)}) %all-to-all-start.6) | async-done | bytes 262176 | tf_op jit(solution)/shard_map/all_to_all | solution.py:302
  144.5 0.9 shard_map.143
  (8 shorter events, 0.0 us)
Async XLA Ops:
  0.6 24.3 %copy-start.7 = (f32[128]{0:T(128)S(1)}, f32[128]{0:T(128)}, u32[]{:S(2)}) copy-start(f32[128]{0:T(128)} %param.11) | copy-start | bytes 1540
  0.6 24.3 %copy-start.8 = (f32[128]{0:T(128)S(1)}, f32[128]{0:T(128)}, u32[]{:S(2)}) copy-start(f32[128]{0:T(128)} %param.14) | copy-start | bytes 1540
  1.4 0.9 copy-start
  2.3 0.9 copy-start.2
  3.2 0.7 copy-start.6
  3.9 21.1 %copy-start.1 = (bf16[128,512]{1,0:T(8,128)(2,1)S(1)}, bf16[128,512]{1,0:T(8,128)(2,1)}, u32[]{:S(2)}) copy-start(bf16[128,512]{1,0:T(8,128)(2,1)} %proj_ref.7) | copy-start | bytes 393220
  3.9 21.1 %copy-start.3 = (bf16[1,6,96,128]{3,2,1,0:T(8,128)(2,1)S(1)}, bf16[1,6,96,128]{3,2,1,0:T(8,128)(2,1)}, u32[]{:S(2)}) copy-start(bf16[1,6,96,128]{3,2,1,0:T(8,128)(2,1)} %param.8) | copy-start | bytes 442372
  3.9 21.1 %copy-start.4 = (bf16[128,128]{1,0:T(8,128)(2,1)S(1)}, bf16[128,128]{1,0:T(8,128)(2,1)}, u32[]{:S(2)}) copy-start(bf16[128,128]{1,0:T(8,128)(2,1)} %gate_ref.5) | copy-start | bytes 98308
  3.9 21.1 %copy-start.5 = (bf16[128,128]{1,0:T(8,128)(2,1)S(1)}, bf16[128,128]{1,0:T(8,128)(2,1)}, u32[]{:S(2)}) copy-start(bf16[128,128]{1,0:T(8,128)(2,1)} %out_weight_ref.5) | copy-start | bytes 98308
  3.9 21.1 %copy-start.11 = (bf16[1,6,96,128]{3,2,1,0:T(8,128)(2,1)S(1)}, bf16[1,6,96,128]{3,2,1,0:T(8,128)(2,1)}, u32[]{:S(2)}) copy-start(bf16[1,6,96,128]{3,2,1,0:T(8,128)(2,1)} %param.9) | copy-start | bytes 442372
  21.4 10.5 %all-to-all-start.1 = ((bf16[16,48,128]{2,1,0:T(8,128)(2,1)}), bf16[16,48,128]{2,1,0:T(8,128)(2,1)S(1)}, u32[]{:S(2)}, u32[]{:S(2)}) async-start(bf16[16,48,128]{2,1,0:T(8,128)(2,1)} %shard_map.136), calls=%async_computation.1 | async-start | bytes 393216 | tf_op jit(solution)/shard_map/all_to_all | solution.py:302
  26.8 0.8 copy-start.12
  27.6 0.7 copy-start.14
  43.6 13.2 %all-to-all-start.3 = ((bf16[16,96,128]{2,1,0:T(8,128)(2,1)}), bf16[16,96,128]{2,1,0:T(8,128)(2,1)S(1)}, u32[]{:S(2)}, u32[]{:S(2)}) async-start(bf16[16,96,128]{2,1,0:T(8,128)(2,1)} %shard_map.140), calls=%async_computation.3 | async-start | bytes 786432 | tf_op jit(solution)/shard_map/all_to_all | solution.py:302
  47.5 1.0 copy-start.13
  48.5 1.0 copy-start.15
  57.3 0.9 copy-start.9
  58.1 77.1 %copy-start.10 = (bf16[6,512,128]{2,1,0:T(8,128)(2,1)S(1)}, bf16[6,512,128]{2,1,0:T(8,128)(2,1)}, u32[]{:S(2)}) copy-start(bf16[6,512,128]{2,1,0:T(8,128)(2,1)} %copy-done.9) | copy-start | bytes 2359300
  127.7 16.8 %all-to-all-start.6 = ((bf16[64,16,128]{2,1,0:T(8,128)(2,1)}), bf16[64,16,128]{2,1,0:T(8,128)(2,1)S(1)}, u32[]{:S(2)}, u32[]{:S(2)}) async-start(bf16[64,16,128]{2,1,0:T(8,128)(2,1)} %broadcast_in_dim.29), calls=%async_computation.6 | async-start | bytes 524288 | tf_op jit(solution)/shard_map/all_to_all | solution.py:302

commit v3 on v2

--- a/solution.py
+++ b/solution.py
@@ -11,6 +11,7 @@
 NEAR = ("zl", "core", "tile")
 LANES = 128
 EPS = 1e-05
+VMEM_BYTES = 16 * 1024 * 1024
 F32 = jnp.float32
 BF16 = jnp.bfloat16
 
@@ -209,28 +210,30 @@
     out_ref[:, half:, :] = right_out[...].astype(BF16).reshape(shape)
 
 
-def proj_grad_kernel(back_ref, factor_ref, normed_ref, grads_ref, lin_ref, out_ref, rows_ref):
+def grad_linear(factor_ref, i, left, right):
+    width = left.shape[0]
+    return jnp.concatenate(
+        [
+            (left * factor_ref[i, :width]).astype(BF16),
+            (left * factor_ref[i, width : 2 * width]).astype(BF16),
+            (right * factor_ref[i, 2 * width : 3 * width]).astype(BF16),
+            (right * factor_ref[i, 3 * width :]).astype(BF16),
+        ],
+        axis=0,
+    )
+
+
+def proj_grad_kernel(back_ref, factor_ref, normed_ref, grads_ref, out_ref, rows_ref):
     rows, wide, _ = factor_ref.shape
     half = back_ref.shape[1] // 2
     size = half // (rows // 2)
-    width = wide // 4
     near, piece, _ = out_ref.shape
     proj_sum = jnp.zeros((wide, normed_ref.shape[2]), F32)
     for pair in range(rows // 2):
         lefts = get_panel(back_ref, 0, pair, size)
         rights = get_panel(back_ref, half, pair, size)
         for i, left, right in zip((2 * pair, 2 * pair + 1), lefts, rights):
-            lin = jnp.concatenate(
-                [
-                    (left * factor_ref[i, :width]).astype(BF16),
-                    (left * factor_ref[i, width : 2 * width]).astype(BF16),
-                    (right * factor_ref[i, 2 * width : 3 * width]).astype(BF16),
-                    (right * factor_ref[i, 3 * width :]).astype(BF16),
-                ],
-                axis=0,
-            )
-            lin_ref[i] = lin
-            proj_sum += mat(lin, normed_ref[i])
+            proj_sum += mat(grad_linear(factor_ref, i, left, right), normed_ref[i])
     main = wide // near
     extra = grads_ref.shape[0] // near
     rows_ref[...] = jnp.zeros(rows_ref.shape, F32)
@@ -242,19 +245,25 @@
 
 
 def pair_grad_kernel(
-    rep_ref, cot_ref, lin_ref, grad_gate_ref, gain_ref, proj_ref, gate_ref, out_ref
+    rep_ref, cot_ref, back_ref, factor_ref, grad_gate_ref, gain_ref, proj_ref, gate_ref, out_ref
 ):
     rows, residues, _ = rep_ref.shape
+    half = back_ref.shape[1] // 2
+    size = half // (rows // 2)
     proj = proj_ref[...]
     gate = gate_ref[...]
     gain = gain_ref[...]
-    for i in range(rows):
-        grad = (mat(proj, lin_ref[i]) + mat(gate, grad_gate_ref[i])).T[:residues] * gain
-        scaled, inverse = row_norm(rep_ref[i].astype(F32))
-        first_mean = jnp.mean(grad, axis=1, keepdims=True)
-        second_mean = jnp.mean(grad * scaled, axis=1, keepdims=True)
-        change = inverse * (grad - first_mean - scaled * second_mean)
-        out_ref[i] = (cot_ref[i].astype(F32) + change).astype(BF16)
+    for pair in range(rows // 2):
+        lefts = get_panel(back_ref, 0, pair, size)
+        rights = get_panel(back_ref, half, pair, size)
+        for i, left, right in zip((2 * pair, 2 * pair + 1), lefts, rights):
+            lin = grad_linear(factor_ref, i, left, right)
+            grad = (mat(proj, lin) + mat(gate, grad_gate_ref[i])).T[:residues] * gain
+            scaled, inverse = row_norm(rep_ref[i].astype(F32))
+            first_mean = jnp.mean(grad, axis=1, keepdims=True)
+            second_mean = jnp.mean(grad * scaled, axis=1, keepdims=True)
+            change = inverse * (grad - first_mean - scaled * second_mean)
+            out_ref[i] = (cot_ref[i].astype(F32) + change).astype(BF16)
 
 
 def final_kernel(
@@ -293,7 +302,7 @@
         in_specs=[pl.BlockSpec(memory_space=pltpu.SMEM)] * smem + [vmem] * (len(args) - smem),
         out_specs=[vmem] * len(shapes),
         scratch_shapes=[pltpu.VMEM(shape, F32) for shape in scratch],
-        compiler_params=pltpu.CompilerParams(vmem_limit_bytes=32 * 1024 * 1024),
+        compiler_params=pltpu.CompilerParams(vmem_limit_bytes=VMEM_BYTES),
         cost_estimate=pl.CostEstimate(flops=flops, bytes_accessed=size, transcendentals=0),
     )(*args)
 
@@ -313,7 +322,6 @@
 def body(pair_rep, cotangent, lengths, in_gain, projections, gate_weight, out_gain, out_weight):
     tiles = lax.axis_size("tile")
     near = lax.axis_size(NEAR)
-    far = lax.axis_size("zh")
     rep, cot = pair_rep[0], cotangent[0]
     rows, residues, chans = rep.shape
     wide = projections.shape[1]
@@ -356,16 +364,16 @@
     )
     back_rows = exchange(back, "tile")
     piece = -(-(wide + 2 * chans) // near // 16) * 16
-    lin, pieces = call(
-        proj_grad_kernel, [((rows, wide, LANES), BF16), ((near, piece, LANES), BF16)],
+    (pieces,) = call(
+        proj_grad_kernel, [((near, piece, LANES), BF16)],
         back_rows, factor, normed, grads, scratch=[(near * piece, LANES)],
     )
     part = total(exchange(pieces, NEAR))
     (pair_grad,) = call(
-        pair_grad_kernel, [(rep.shape, BF16)], rep, cot, lin, grad_gate, gain, projections,
-        gate_weight, flops=10**9,
-    )
-    whole = total(exchange(spread(part, far), "zh"))
+        pair_grad_kernel, [(rep.shape, BF16)], rep, cot, back_rows, factor, grad_gate, gain,
+        projections, gate_weight, flops=10**9,
+    )
+    whole = total(lax.all_gather(part, "zh"))
     sums = exchange(spread(whole, near), NEAR)
     proj_grad, gate_grad, out_grad, gain_grad, gain_o_grad = call(
         final_kernel,

time: 146 us -> 140 us (0.959)
  blocking collectives: 94.2 us -> 85.2 us
  starting transfers between devices: 14.9 us -> 19.3 us
    all_to_all x4 -> x3, blocking collectives: 94.2 us -> 53.7 us  [exchange(): return lax.all_to_all(pieces, axes, split_axis=0, concat_axis=0, tiled=True)]
    all_gather x0 -> x1, blocking collectives: none -> 31.5 us  [body(): whole = total(lax.all_gather(part, 'zh'))]
    all_to_all x3, starting transfers between devices: 14.9 us -> 19.3 us  [exchange(): return lax.all_to_all(pieces, axes, split_axis=0, concat_axis=0, tiled=True)]
    unnamed x32 -> x28, local copies, waits for them, and re-layouts: 6.85 us -> 5.98 us
  transfers between devices with their start and end apart: 3 -> 3, of which waited for: 3 -> 3; matrix products, arithmetic and copies ran while one was open for 0% -> 0% of each run, Pallas kernels for 3% -> 4%
where the time goes in v3:
time: 140 us; the launch traced here: 139 us
  blocking collectives  85.2 us (61%)
  starting transfers between devices  19.3 us (14%)
  waiting for transfers between devices  16.5 us (12%)
  Pallas kernels  10.1 us (7%)
  local copies, waits for them, and re-layouts  6.71 us (5%)
  between operations  1.47 us (1%)
    all_to_all x3, blocking collectives, exchange(): return lax.all_to_all(pieces, axes, split_axis=0, concat_axis=0, tiled=True)  53.7 us
    all_gather x1, blocking collectives, body(): whole = total(lax.all_gather(part, 'zh'))  31.5 us
    all_to_all x3, starting transfers between devices, exchange(): return lax.all_to_all(pieces, axes, split_axis=0, concat_axis=0, tiled=True)  19.3 us
    all_to_all x3, waiting for transfers between devices, exchange(): return lax.all_to_all(pieces, axes, split_axis=0, concat_axis=0, tiled=True)  16.5 us
    pallas_call x9, Pallas kernels, call(): pl.pallas_call(kernel, out_shape=shapes, in_specs=[pl.BlockSpec(memory_sp...  10.1 us
    unnamed x28, local copies, waits for them, and re-layouts  5.98 us
  transfers between devices with their start and end apart: 3, of which 3 were waited for; matrix products, arithmetic and copies ran while one was open for 0% of the time, Pallas kernels for 4%

profile of v3, /device:TPU:1, one launch (start us, length us, event | category | flops | bytes accessed | tf_op | source)
XLA Modules:
  0.0 139.4 jit_solution(2025126898473224338)
XLA Ops:
  0.6 0.0 copy-start.7
  0.6 0.0 copy-start.8
  1.3 0.1 pad_add_fusion.info_ref
  1.4 0.0 copy-start
  1.4 0.9 copy-done
  2.3 0.0 copy-start.2
  2.3 0.9 copy-done.2
  3.2 0.0 copy-start.6
  3.2 0.7 copy-done.6
  3.9 0.0 copy-start.1
  3.9 0.0 copy-start.3
  3.9 0.0 copy-start.4
  3.9 0.0 copy-start.5
  3.9 0.0 copy-start.9
  3.9 1.2 shard_map.135
  5.1 15.4 %all_to_all.30.panel_ref = bf16[16,96,128]{2,1,0:T(8,128)(2,1)S(1)} all-to-all(bf16[16,96,128]{2,1,0:T(8,128)(2,1)S(1)} %shard_map.135), channel_id=1, replica_groups=mesh['zh'=16,'zl'=2,'core'=2,'tile'=16] {'tile'}, dimensions={0} | all-to-all | bytes 786432 | tf_op jit(solution)/shard_map/all_to_all | solution.py:311
  20.5 1.0 shard_map.136
  21.4 3.5 %all-to-all-start.1 = ((bf16[16,48,128]{2,1,0:T(8,128)(2,1)}), bf16[16,48,128]{2,1,0:T(8,128)(2,1)S(1)}, u32[]{:S(2)}, u32[]{:S(2)}) async-start(bf16[16,48,128]{2,1,0:T(8,128)(2,1)} %shard_map.136), calls=%async_computation.1 | async-start | bytes 393216 | tf_op jit(solution)/shard_map/all_to_all | solution.py:311
  25.0 0.0 copy-done.7
  25.0 0.0 copy-done.8
  25.0 0.0 copy-done.1
  25.0 0.0 copy-done.3
  25.0 0.0 copy-done.4
  25.0 0.0 copy-done.5
  25.0 0.0 copy-done.9
  25.0 1.8 %shard_map.137 = (bf16[6,128,128]{2,1,0:T(8,128)(2,1)S(1)}, f32[6,512,128]{2,1,0:T(8,128)S(1)}, f32[6,128,128]{2,1,0:T(8,128)S(1)}, bf16[6,128,128]{2,1,0:T(8,12...) custom-call(s32[2]{0:T(128)S(1)} %pad_add_fusion.info_ref, bf16[6,96,128]{2,1,0:T(8,128)(2,1)S(1)} %bitcast.11, ...), custom_call_target="tpu_custom_call" | custom-call | flops 1000000000 | bytes 492552 | tf_op jit(solution)/shard_map/pallas_call | solution.py:299
  26.8 0.0 copy-start.10
  26.8 0.7 copy-done.10
  27.6 0.7 copy-done.12
  28.3 3.6 %all-to-all-done.1.tri_ref = bf16[16,48,128]{2,1,0:T(8,128)(2,1)S(1)} async-done(((bf16[16,48,128]{2,1,0:T(8,128)(2,1)}), bf16[16,48,128]{2,1,0:T(8,128)(2,1)S(1)}, u32[]{:S(2)}, u32[]{:S(2)}) %all-to-all-start.1) | async-done | bytes 196640 | tf_op jit(solution)/shard_map/all_to_all | solution.py:311
  32.0 0.2 shard_map.139
  32.2 10.1 %all_to_all.31.grad_ref = bf16[16,48,128]{2,1,0:T(8,128)(2,1)S(1)} all-to-all(bf16[16,48,128]{2,1,0:T(8,128)(2,1)S(1)} %shard_map.139), channel_id=1, replica_groups=mesh['zh'=16,'zl'=2,'core'=2,'tile'=16] {'tile'}, dimensions={0} | all-to-all | bytes 393216 | tf_op jit(solution)/shard_map/all_to_all | solution.py:311
  42.3 1.2 shard_map.140
  43.6 3.9 %all-to-all-start.3 = ((bf16[16,96,128]{2,1,0:T(8,128)(2,1)}), bf16[16,96,128]{2,1,0:T(8,128)(2,1)S(1)}, u32[]{:S(2)}, u32[]{:S(2)}) async-start(bf16[16,96,128]{2,1,0:T(8,128)(2,1)} %shard_map.140), calls=%async_computation.3 | async-start | bytes 786432 | tf_op jit(solution)/shard_map/all_to_all | solution.py:311
  47.5 0.0 copy-start.11
  47.5 1.0 copy-done.11
  48.5 1.0 copy-done.13
  49.5 1.6 %shard_map.138 = (bf16[6,96,128]{2,1,0:T(8,128)(2,1)}, bf16[6,128,128]{2,1,0:T(8,128)(2,1)S(1)}, f32[256,128]{1,0:T(8,128)S(1)}) custom-call(bf16[6,96,128]{2,1,0:T(8,128)(2,1)S(1)} %bitcast.12, bf16[16,48,128]{2,1,0:T(8,128)(2,1)S(1)} %all-to-all-done.1.tri_ref, bf16[6,128,128]{2,1,0:T(8,128)(2,1)S(1)} %get-tuple-element.21.normed_ref, ...), custom_call_target="tpu_custom_call" | custom-call | flops 1000000000 | bytes 1556992 | tf_op jit(solution)/shard_map/pallas_call | solution.py:299
  51.1 5.3 %all-to-all-done.3.back_ref = bf16[16,96,128]{2,1,0:T(8,128)(2,1)S(1)} async-done(((bf16[16,96,128]{2,1,0:T(8,128)(2,1)}), bf16[16,96,128]{2,1,0:T(8,128)(2,1)S(1)}, u32[]{:S(2)}, u32[]{:S(2)}) %all-to-all-start.3) | async-done | bytes 393248 | tf_op jit(solution)/shard_map/all_to_all | solution.py:311
  56.3 0.5 shard_map.142
  56.8 28.2 %all_to_all.32 = bf16[64,16,128]{2,1,0:T(8,128)(2,1)S(1)} all-to-all(bf16[64,16,128]{2,1,0:T(8,128)(2,1)S(1)} %shard_map.142), channel_id=1, replica_groups=mesh['zh'=16,'zl'=2,'core'=2,'tile'=16] {'zl','core','tile'}, dimensions={0} | all-to-all | bytes 524288 | tf_op jit(solution)/shard_map/all_to_all | solution.py:311
  85.0 0.1 reduce_sum.24
  85.1 31.5 %all-gather = bf16[256,128]{1,0:T(8,128)(2,1)S(1)} all-gather(bf16[16,128]{1,0:T(8,128)(2,1)S(1)} %reduce_sum.24), channel_id=2, replica_groups=mesh['zh'=16,'zl'=2,'core'=2,'tile'=16] {'zh'}, dimensions={0}, use_global_device_ids=true | all-gather | bytes 69632 | tf_op jit(solution)/shard_map/all_gather | solution.py:376
  116.6 0.7 broadcast_in_dim.22
  117.3 11.9 %all-to-all-start.5 = ((bf16[64,16,128]{2,1,0:T(8,128)(2,1)}), bf16[64,16,128]{2,1,0:T(8,128)(2,1)S(1)}, u32[]{:S(2)}, u32[]{:S(2)}) async-start(bf16[64,16,128]{2,1,0:T(8,128)(2,1)} %broadcast_in_dim.22), calls=%async_computation.5 | async-start | bytes 524288 | tf_op jit(solution)/shard_map/all_to_all | solution.py:311
  129.2 1.7 %shard_map.141 = bf16[6,96,128]{2,1,0:T(8,128)(2,1)} custom-call(bf16[6,96,128]{2,1,0:T(8,128)(2,1)S(1)} %bitcast.13, bf16[6,96,128]{2,1,0:T(8,128)(2,1)S(1)} %bitcast.22, bf16[16,96,128]{2,1,0:T(8,128)(2,1)S(1)} %all-to-all-done.3.back_ref, f32[6,512,128]{2,1,0:T(8,128)S(1)} %get-tuple-element.27.factor_ref, ...), custom_call_target="tpu_custom_call" | custom-call | flops 1000000000 | bytes 2621952 | tf_op jit(solution)/shard_map/pallas_call | solution.py:299
  130.9 7.6 %all-to-all-done.5.sum_ref = bf16[64,16,128]{2,1,0:T(8,128)(2,1)S(1)} async-done(((bf16[64,16,128]{2,1,0:T(8,128)(2,1)}), bf16[64,16,128]{2,1,0:T(8,128)(2,1)S(1)}, u32[]{:S(2)}, u32[]{:S(2)}) %all-to-all-start.5) | async-done | bytes 262176 | tf_op jit(solution)/shard_map/all_to_all | solution.py:311
  138.5 0.9 shard_map.143
  (3 shorter events, 0.0 us)
Async XLA Ops:
  0.6 24.3 %copy-start.7 = (f32[128]{0:T(128)S(1)}, f32[128]{0:T(128)}, u32[]{:S(2)}) copy-start(f32[128]{0:T(128)} %param.11) | copy-start | bytes 1540
  0.6 24.3 %copy-start.8 = (f32[128]{0:T(128)S(1)}, f32[128]{0:T(128)}, u32[]{:S(2)}) copy-start(f32[128]{0:T(128)} %param.14) | copy-start | bytes 1540
  1.4 0.9 copy-start
  2.3 0.9 copy-start.2
  3.2 0.7 copy-start.6
  3.9 21.1 %copy-start.1 = (bf16[128,512]{1,0:T(8,128)(2,1)S(1)}, bf16[128,512]{1,0:T(8,128)(2,1)}, u32[]{:S(2)}) copy-start(bf16[128,512]{1,0:T(8,128)(2,1)} %proj_ref.7) | copy-start | bytes 393220
  3.9 21.1 %copy-start.3 = (bf16[1,6,96,128]{3,2,1,0:T(8,128)(2,1)S(1)}, bf16[1,6,96,128]{3,2,1,0:T(8,128)(2,1)}, u32[]{:S(2)}) copy-start(bf16[1,6,96,128]{3,2,1,0:T(8,128)(2,1)} %param.8) | copy-start | bytes 442372
  3.9 21.1 %copy-start.4 = (bf16[128,128]{1,0:T(8,128)(2,1)S(1)}, bf16[128,128]{1,0:T(8,128)(2,1)}, u32[]{:S(2)}) copy-start(bf16[128,128]{1,0:T(8,128)(2,1)} %gate_ref.5) | copy-start | bytes 98308
  3.9 21.1 %copy-start.5 = (bf16[128,128]{1,0:T(8,128)(2,1)S(1)}, bf16[128,128]{1,0:T(8,128)(2,1)}, u32[]{:S(2)}) copy-start(bf16[128,128]{1,0:T(8,128)(2,1)} %out_weight_ref.5) | copy-start | bytes 98308
  3.9 21.1 %copy-start.9 = (bf16[1,6,96,128]{3,2,1,0:T(8,128)(2,1)S(1)}, bf16[1,6,96,128]{3,2,1,0:T(8,128)(2,1)}, u32[]{:S(2)}) copy-start(bf16[1,6,96,128]{3,2,1,0:T(8,128)(2,1)} %param.9) | copy-start | bytes 442372
  21.4 10.5 %all-to-all-start.1 = ((bf16[16,48,128]{2,1,0:T(8,128)(2,1)}), bf16[16,48,128]{2,1,0:T(8,128)(2,1)S(1)}, u32[]{:S(2)}, u32[]{:S(2)}) async-start(bf16[16,48,128]{2,1,0:T(8,128)(2,1)} %shard_map.136), calls=%async_computation.1 | async-start | bytes 393216 | tf_op jit(solution)/shard_map/all_to_all | solution.py:311
  26.8 0.8 copy-start.10
  27.6 0.7 copy-start.12
  43.6 12.8 %all-to-all-start.3 = ((bf16[16,96,128]{2,1,0:T(8,128)(2,1)}), bf16[16,96,128]{2,1,0:T(8,128)(2,1)S(1)}, u32[]{:S(2)}, u32[]{:S(2)}) async-start(bf16[16,96,128]{2,1,0:T(8,128)(2,1)} %shard_map.140), calls=%async_computation.3 | async-start | bytes 786432 | tf_op jit(solution)/shard_map/all_to_all | solution.py:311
  47.5 1.0 copy-start.11
  48.5 1.0 copy-start.13
  117.3 21.2 %all-to-all-start.5 = ((bf16[64,16,128]{2,1,0:T(8,128)(2,1)}), bf16[64,16,128]{2,1,0:T(8,128)(2,1)S(1)}, u32[]{:S(2)}, u32[]{:S(2)}) async-start(bf16[64,16,128]{2,1,0:T(8,128)(2,1)} %broadcast_in_dim.22), calls=%async_computation.5 | async-start | bytes 524288 | tf_op jit(solution)/shard_map/all_to_all | solution.py:311

commit v4 on v3

--- a/solution.py
+++ b/solution.py
@@ -12,6 +12,7 @@
 LANES = 128
 EPS = 1e-05
 VMEM_BYTES = 16 * 1024 * 1024
+LARGE_VMEM_BYTES = 56 * 1024 * 1024
 F32 = jnp.float32
 BF16 = jnp.bfloat16
 
@@ -45,10 +46,11 @@
     return pad_rows((scaled * gain).astype(BF16), LANES)
 
 
-def masks(info_ref, i):
+def masks(info_ref, rows, i):
     length = info_ref[0]
+    first = lax.axis_index("tile") * rows
     lane = lax.broadcasted_iota(jnp.int32, (1, LANES), 1)
-    inside = jnp.logical_and(lane < length, info_ref[1] + i < length)
+    inside = jnp.logical_and(lane < length, first + i < length)
     return inside.astype(F32)
 
 
@@ -76,7 +78,18 @@
     return both[:, :half].reshape(-1, LANES), both[:, half:].reshape(-1, LANES)
 
 
-def panels_kernel(info_ref, rep_ref, gain_ref, proj_ref, out_ref):
+def panels_kernel(
+    info_ref, rep_hbm, gain_hbm, proj_hbm, out_ref, rep_ref, gain_ref, proj_ref, sem
+):
+    copies = [
+        pltpu.make_async_copy(proj_hbm, proj_ref, sem.at[0]),
+        pltpu.make_async_copy(rep_hbm, rep_ref, sem.at[1]),
+        pltpu.make_async_copy(gain_hbm, gain_ref, sem.at[2]),
+    ]
+    for copy in copies:
+        copy.start()
+    for copy in copies:
+        copy.wait()
     rows = rep_ref.shape[0]
     width = proj_ref.shape[1] // 4
     half = out_ref.shape[1] // 2
@@ -87,7 +100,7 @@
         for i in (2 * pair, 2 * pair + 1):
             linear = mat_nt(proj, normed_row(rep_ref, gain, i))
             lin_left, sig_left, lin_right, sig_right = gated(linear, width)
-            mask = masks(info_ref, i)
+            mask = masks(info_ref, rows, i)
             left.append(sig_left * lin_left * mask)
             right.append(sig_right * lin_right * mask)
         put_panel(out_ref, 0, pair, *left)
@@ -109,7 +122,7 @@
         normed = normed_row(rep_ref, gain, i)
         normed_ref[i] = normed
         lin_left, sig_left, lin_right, sig_right = gated(mat_nt(proj, normed), width)
-        mask = masks(info_ref, i)
+        mask = masks(info_ref, rows, i)
         factor_ref[i, :width] = sig_left * mask
         factor_ref[i, width : 2 * width] = lin_left * mask * sig_left * (1.0 - sig_left)
         factor_ref[i, 2 * width : 3 * width] = sig_right * mask
@@ -292,17 +305,22 @@
     out_gain_grad_ref[...] = jnp.broadcast_to(outs, (chans, LANES)).T[:1] / out_gain_ref[...]
 
 
-def call(kernel, outs, *args, smem=0, scratch=(), flops=0):
+def call(kernel, outs, *args, smem=0, scratch=(), flops=0, staged=False):
     vmem = pl.BlockSpec(memory_space=pltpu.VMEM)
     size = sum(a.size * a.dtype.itemsize for a in args)
     shapes = [jax.ShapeDtypeStruct(shape, dtype) for shape, dtype in outs]
     return pl.pallas_call(
         kernel,
         out_shape=shapes,
-        in_specs=[pl.BlockSpec(memory_space=pltpu.SMEM)] * smem + [vmem] * (len(args) - smem),
+        in_specs=[pl.BlockSpec(memory_space=pltpu.SMEM)] * smem + [pl.BlockSpec(memory_space=pl.ANY) if staged else vmem] * (len(args) - smem),
         out_specs=[vmem] * len(shapes),
-        scratch_shapes=[pltpu.VMEM(shape, F32) for shape in scratch],
-        compiler_params=pltpu.CompilerParams(vmem_limit_bytes=VMEM_BYTES),
+        scratch_shapes=(
+            [pltpu.VMEM(a.shape, a.dtype) for a in args[smem:]]
+            + [pltpu.SemaphoreType.DMA((len(args) - smem,))]
+            if staged
+            else [pltpu.VMEM(shape, F32) for shape in scratch]
+        ),
+        compiler_params=pltpu.CompilerParams(vmem_limit_bytes=LARGE_VMEM_BYTES if staged else VMEM_BYTES),
         cost_estimate=pl.CostEstimate(flops=flops, bytes_accessed=size, transcendentals=0),
     )(*args)
 
@@ -328,12 +346,13 @@
     width = wide // 4
     panel = rows * width // tiles
     lines = residues * width // tiles
-    info = jnp.stack([lengths[0], lax.axis_index("tile") * rows])
+    info = lengths
     gain, gain_o = in_gain[None], out_gain[None]
     grid = (rows, LANES, LANES)
 
     (panels,) = call(
-        panels_kernel, [((tiles, 2 * panel, LANES), BF16)], info, rep, gain, projections, smem=1
+        panels_kernel, [((tiles, 2 * panel, LANES), BF16)], info, rep, gain, projections, smem=1,
+        staged=True,
     )
     sides = exchange(panels, "tile")
     normed, factor, sig, update, slope, upstream = call(

time: 140 us -> 139 us (level)
  local copies, waits for them, and re-layouts: 6.71 us -> 4.24 us
    unnamed x28 -> x22, local copies, waits for them, and re-layouts: 5.98 us -> 3.51 us
  transfers between devices with their start and end apart: 3 -> 3, of which waited for: 3 -> 3; matrix products, arithmetic and copies ran while one was open for 0% -> 0% of each run, Pallas kernels for 4% -> 3%
where the time goes in v4:
time: 139 us; the launch traced here: 138 us
  blocking collectives  86 us (62%)
  starting transfers between devices  18.9 us (14%)
  waiting for transfers between devices  16.7 us (12%)
  Pallas kernels  10.8 us (8%)
  local copies, waits for them, and re-layouts  4.24 us (3%)
  between operations  1.57 us (1%)
    all_to_all x3, blocking collectives, exchange(): return lax.all_to_all(pieces, axes, split_axis=0, concat_axis=0, tiled=True)  54.5 us
    all_gather x1, blocking collectives, body(): whole = total(lax.all_gather(part, 'zh'))  31.5 us
    all_to_all x3, starting transfers between devices, exchange(): return lax.all_to_all(pieces, axes, split_axis=0, concat_axis=0, tiled=True)  18.9 us
    all_to_all x3, waiting for transfers between devices, exchange(): return lax.all_to_all(pieces, axes, split_axis=0, concat_axis=0, tiled=True)  16.7 us
    pallas_call x9, Pallas kernels, call(): pl.pallas_call(kernel, out_shape=shapes, in_specs=[pl.BlockSpec(memory_sp...  10.8 us
    unnamed x22, local copies, waits for them, and re-layouts  3.51 us
  transfers between devices with their start and end apart: 3, of which 3 were waited for; matrix products, arithmetic and copies ran while one was open for 0% of the time, Pallas kernels for 3%

profile of v4, /device:TPU:1, one launch (start us, length us, event | category | flops | bytes accessed | tf_op | source)
XLA Modules:
  0.0 138.4 jit_solution(10189218868030004625)
XLA Ops:
  0.6 0.0 copy-start
  0.6 0.0 copy-start.4
  0.7 0.0 copy-start.1
  0.7 0.0 copy-start.3
  0.7 0.0 copy-start.2
  0.7 0.0 copy-start.5
  0.7 0.0 copy-start.6
  1.5 2.4 %shard_map.135 = bf16[16,96,128]{2,1,0:T(8,128)(2,1)} custom-call(s32[1]{0:T(128)S(6)} %copy.15.info_ref, bf16[6,96,128]{2,1,0:T(8,128)(2,1)} %bitcast.9, f32[1,128]{1,0:T(1,128)} %bitcast.13, bf16[128,512]{1,0:T(8,128)(2,1)} %proj_ref.5), custom_call_target="tpu_custom_call" | custom-call | bytes 279044 | tf_op jit(solution)/shard_map/pallas_call | solution.py:312
  3.9 15.6 %all_to_all.30.panel_ref = bf16[16,96,128]{2,1,0:T(8,128)(2,1)S(1)} all-to-all(bf16[16,96,128]{2,1,0:T(8,128)(2,1)} %shard_map.135), channel_id=1, replica_groups=mesh['zh'=16,'zl'=2,'core'=2,'tile'=16] {'tile'}, dimensions={0} | all-to-all | bytes 786432 | tf_op jit(solution)/shard_map/all_to_all | solution.py:329
  19.4 1.0 shard_map.136
  20.4 3.5 %all-to-all-start.1 = ((bf16[16,48,128]{2,1,0:T(8,128)(2,1)}), bf16[16,48,128]{2,1,0:T(8,128)(2,1)S(1)}, u32[]{:S(2)}, u32[]{:S(2)}) async-start(bf16[16,48,128]{2,1,0:T(8,128)(2,1)} %shard_map.136), calls=%async_computation.1 | async-start | bytes 393216 | tf_op jit(solution)/shard_map/all_to_all | solution.py:329
  23.9 0.0 copy-done
  23.9 0.0 copy-done.4
  24.0 0.0 copy-done.1
  24.0 0.0 copy-done.3
  24.0 0.0 copy-done.2
  24.0 0.0 copy-done.5
  24.0 0.0 copy-done.6
  24.0 1.2 shard_map.137
  25.3 0.0 copy-start.7
  25.3 0.7 copy-done.7
  26.0 0.0 copy-start.9
  26.0 0.8 copy-done.9
  26.8 4.4 %all-to-all-done.1.tri_ref = bf16[16,48,128]{2,1,0:T(8,128)(2,1)S(1)} async-done(((bf16[16,48,128]{2,1,0:T(8,128)(2,1)}), bf16[16,48,128]{2,1,0:T(8,128)(2,1)S(1)}, u32[]{:S(2)}, u32[]{:S(2)}) %all-to-all-start.1) | async-done | bytes 196640 | tf_op jit(solution)/shard_map/all_to_all | solution.py:329
  31.1 0.2 shard_map.139
  31.4 10.2 %all_to_all.31.grad_ref = bf16[16,48,128]{2,1,0:T(8,128)(2,1)S(1)} all-to-all(bf16[16,48,128]{2,1,0:T(8,128)(2,1)S(1)} %shard_map.139), channel_id=1, replica_groups=mesh['zh'=16,'zl'=2,'core'=2,'tile'=16] {'tile'}, dimensions={0} | all-to-all | bytes 393216 | tf_op jit(solution)/shard_map/all_to_all | solution.py:329
  41.6 1.2 shard_map.140
  42.8 3.6 %all-to-all-start.3 = ((bf16[16,96,128]{2,1,0:T(8,128)(2,1)}), bf16[16,96,128]{2,1,0:T(8,128)(2,1)S(1)}, u32[]{:S(2)}, u32[]{:S(2)}) async-start(bf16[16,96,128]{2,1,0:T(8,128)(2,1)} %shard_map.140), calls=%async_computation.3 | async-start | bytes 786432 | tf_op jit(solution)/shard_map/all_to_all | solution.py:329
  46.4 0.0 copy-start.8
  46.4 1.0 copy-done.8
  47.4 0.0 copy-start.10
  47.4 1.0 copy-done.10
  48.4 1.6 %shard_map.138 = (bf16[6,96,128]{2,1,0:T(8,128)(2,1)}, bf16[6,128,128]{2,1,0:T(8,128)(2,1)S(1)}, f32[256,128]{1,0:T(8,128)S(1)}) custom-call(bf16[6,96,128]{2,1,0:T(8,128)(2,1)S(1)} %bitcast.11, bf16[16,48,128]{2,1,0:T(8,128)(2,1)S(1)} %all-to-all-done.1.tri_ref, bf16[6,128,128]{2,1,0:T(8,128)(2,1)S(1)} %get-tuple-element.21.normed_ref, ...), custom_call_target="tpu_custom_call" | custom-call | flops 1000000000 | bytes 1556992 | tf_op jit(solution)/shard_map/pallas_call | solution.py:312
  50.0 4.8 %all-to-all-done.3.back_ref = bf16[16,96,128]{2,1,0:T(8,128)(2,1)S(1)} async-done(((bf16[16,96,128]{2,1,0:T(8,128)(2,1)}), bf16[16,96,128]{2,1,0:T(8,128)(2,1)S(1)}, u32[]{:S(2)}, u32[]{:S(2)}) %all-to-all-start.3) | async-done | bytes 393248 | tf_op jit(solution)/shard_map/all_to_all | solution.py:329
  54.7 0.5 shard_map.142
  55.2 28.7 %all_to_all.32 = bf16[64,16,128]{2,1,0:T(8,128)(2,1)S(1)} all-to-all(bf16[64,16,128]{2,1,0:T(8,128)(2,1)S(1)} %shard_map.142), channel_id=1, replica_groups=mesh['zh'=16,'zl'=2,'core'=2,'tile'=16] {'zl','core','tile'}, dimensions={0} | all-to-all | bytes 524288 | tf_op jit(solution)/shard_map/all_to_all | solution.py:329
  83.9 0.1 reduce_sum.24
  84.0 31.5 %all-gather = bf16[256,128]{1,0:T(8,128)(2,1)S(1)} all-gather(bf16[16,128]{1,0:T(8,128)(2,1)S(1)} %reduce_sum.24), channel_id=2, replica_groups=mesh['zh'=16,'zl'=2,'core'=2,'tile'=16] {'zh'}, dimensions={0}, use_global_device_ids=true | all-gather | bytes 69632 | tf_op jit(solution)/shard_map/all_gather | solution.py:395
  115.5 0.7 broadcast_in_dim.22
  116.3 11.9 %all-to-all-start.5 = ((bf16[64,16,128]{2,1,0:T(8,128)(2,1)}), bf16[64,16,128]{2,1,0:T(8,128)(2,1)S(1)}, u32[]{:S(2)}, u32[]{:S(2)}) async-start(bf16[64,16,128]{2,1,0:T(8,128)(2,1)} %broadcast_in_dim.22), calls=%async_computation.5 | async-start | bytes 524288 | tf_op jit(solution)/shard_map/all_to_all | solution.py:329
  128.1 1.7 %shard_map.141 = bf16[6,96,128]{2,1,0:T(8,128)(2,1)} custom-call(bf16[6,96,128]{2,1,0:T(8,128)(2,1)S(1)} %bitcast.12, bf16[6,96,128]{2,1,0:T(8,128)(2,1)S(1)} %bitcast.21, bf16[16,96,128]{2,1,0:T(8,128)(2,1)S(1)} %all-to-all-done.3.back_ref, f32[6,512,128]{2,1,0:T(8,128)S(1)} %get-tuple-element.27.factor_ref, ...), custom_call_target="tpu_custom_call" | custom-call | flops 1000000000 | bytes 2621952 | tf_op jit(solution)/shard_map/pallas_call | solution.py:312
  129.9 7.6 %all-to-all-done.5.sum_ref = bf16[64,16,128]{2,1,0:T(8,128)(2,1)S(1)} async-done(((bf16[64,16,128]{2,1,0:T(8,128)(2,1)}), bf16[64,16,128]{2,1,0:T(8,128)(2,1)S(1)}, u32[]{:S(2)}, u32[]{:S(2)}) %all-to-all-start.5) | async-done | bytes 262176 | tf_op jit(solution)/shard_map/all_to_all | solution.py:329
  137.5 0.9 shard_map.143
  (1 shorter events, 0.0 us)
Async XLA Ops:
  0.6 23.3 %copy-start = (bf16[128,512]{1,0:T(8,128)(2,1)S(1)}, bf16[128,512]{1,0:T(8,128)(2,1)}, u32[]{:S(2)}) copy-start(bf16[128,512]{1,0:T(8,128)(2,1)} %proj_ref.5) | copy-start | bytes 393220
  0.6 23.3 %copy-start.4 = (f32[128]{0:T(128)S(1)}, f32[128]{0:T(128)}, u32[]{:S(2)}) copy-start(f32[128]{0:T(128)} %param.11) | copy-start | bytes 1540
  0.7 23.3 %copy-start.1 = (bf16[1,6,96,128]{3,2,1,0:T(8,128)(2,1)S(1)}, bf16[1,6,96,128]{3,2,1,0:T(8,128)(2,1)}, u32[]{:S(2)}) copy-start(bf16[1,6,96,128]{3,2,1,0:T(8,128)(2,1)} %param.8) | copy-start | bytes 442372
  0.7 23.3 %copy-start.3 = (bf16[128,128]{1,0:T(8,128)(2,1)S(1)}, bf16[128,128]{1,0:T(8,128)(2,1)}, u32[]{:S(2)}) copy-start(bf16[128,128]{1,0:T(8,128)(2,1)} %out_weight_ref.5) | copy-start | bytes 98308
  0.7 23.3 %copy-start.2 = (bf16[128,128]{1,0:T(8,128)(2,1)S(1)}, bf16[128,128]{1,0:T(8,128)(2,1)}, u32[]{:S(2)}) copy-start(bf16[128,128]{1,0:T(8,128)(2,1)} %gate_ref.5) | copy-start | bytes 98308
  0.7 23.3 %copy-start.5 = (f32[128]{0:T(128)S(1)}, f32[128]{0:T(128)}, u32[]{:S(2)}) copy-start(f32[128]{0:T(128)} %param.14) | copy-start | bytes 1540
  0.7 23.3 %copy-start.6 = (bf16[1,6,96,128]{3,2,1,0:T(8,128)(2,1)S(1)}, bf16[1,6,96,128]{3,2,1,0:T(8,128)(2,1)}, u32[]{:S(2)}) copy-start(bf16[1,6,96,128]{3,2,1,0:T(8,128)(2,1)} %param.9) | copy-start | bytes 442372
  20.4 10.7 %all-to-all-start.1 = ((bf16[16,48,128]{2,1,0:T(8,128)(2,1)}), bf16[16,48,128]{2,1,0:T(8,128)(2,1)S(1)}, u32[]{:S(2)}, u32[]{:S(2)}) async-start(bf16[16,48,128]{2,1,0:T(8,128)(2,1)} %shard_map.136), calls=%async_computation.1 | async-start | bytes 393216 | tf_op jit(solution)/shard_map/all_to_all | solution.py:329
  25.3 0.7 copy-start.7
  26.0 0.8 copy-start.9
  42.8 11.9 %all-to-all-start.3 = ((bf16[16,96,128]{2,1,0:T(8,128)(2,1)}), bf16[16,96,128]{2,1,0:T(8,128)(2,1)S(1)}, u32[]{:S(2)}, u32[]{:S(2)}) async-start(bf16[16,96,128]{2,1,0:T(8,128)(2,1)} %shard_map.140), calls=%async_computation.3 | async-start | bytes 786432 | tf_op jit(solution)/shard_map/all_to_all | solution.py:329
  46.4 1.0 copy-start.8
  47.4 1.0 copy-start.10
  116.3 21.2 %all-to-all-start.5 = ((bf16[64,16,128]{2,1,0:T(8,128)(2,1)}), bf16[64,16,128]{2,1,0:T(8,128)(2,1)S(1)}, u32[]{:S(2)}, u32[]{:S(2)}) async-start(bf16[64,16,128]{2,1,0:T(8,128)(2,1)} %broadcast_in_dim.22), calls=%async_computation.5 | async-start | bytes 524288 | tf_op jit(solution)/shard_map/all_to_all | solution.py:329

commit v5 on v4

--- a/solution.py
+++ b/solution.py
@@ -63,6 +63,43 @@
     )
 
 
+def pack(a, b, c, d):
+    used = LANES * 3 // 4
+    third = used // 3
+    free = lax.broadcasted_iota(jnp.int32, (1, LANES), 1) >= used
+    return tuple(
+        jnp.where(free, pltpu.roll(d, used - m * third, 1), block)
+        for m, block in enumerate((a, b, c))
+    )
+
+
+def unpack(a, b, c):
+    used = LANES * 3 // 4
+    third = used // 3
+    lane = lax.broadcasted_iota(jnp.int32, (1, LANES), 1)
+    zero = jnp.zeros_like(a)
+    d = zero
+    for m, block in reversed(list(enumerate((a, b, c)))):
+        place = jnp.logical_and(lane >= m * third, lane < (m + 1) * third)
+        d = jnp.where(place, pltpu.roll(block, third * (m + 1), 1), d)
+    return tuple(jnp.where(lane < used, block, zero) for block in (a, b, c)) + (d,)
+
+
+def put_packed(pack_ref, pair, blocks):
+    peers = pack_ref.shape[0]
+    for m, block in enumerate(pack(*blocks)):
+        block = block.reshape(peers, -1, LANES)
+        size = block.shape[1]
+        start = (3 * pair + m) * size
+        pack_ref[:, start : start + size, :] = block
+
+
+def get_packed(pack_ref, pair, pairs):
+    size = pack_ref.shape[1] // (3 * pairs)
+    starts = [(3 * pair + m) * size for m in range(3)]
+    return unpack(*(pack_ref[:, s : s + size, :].reshape(-1, LANES) for s in starts))
+
+
 def put_panel(out_ref, start, pair, first, second):
     peers = out_ref.shape[0]
     first = first.reshape(peers, -1, LANES)
@@ -79,7 +116,7 @@
 
 
 def panels_kernel(
-    info_ref, rep_hbm, gain_hbm, proj_hbm, out_ref, rep_ref, gain_ref, proj_ref, sem
+    info_ref, rep_hbm, gain_hbm, proj_hbm, out_ref, rep_ref, gain_ref, proj_ref, sem, pack_ref
 ):
     copies = [
         pltpu.make_async_copy(proj_hbm, proj_ref, sem.at[0]),
@@ -92,7 +129,6 @@
         copy.wait()
     rows = rep_ref.shape[0]
     width = proj_ref.shape[1] // 4
-    half = out_ref.shape[1] // 2
     proj = flip(proj_ref[...])
     gain = gain_ref[...]
     for pair in range(rows // 2):
@@ -103,8 +139,8 @@
             mask = masks(info_ref, rows, i)
             left.append(sig_left * lin_left * mask)
             right.append(sig_right * lin_right * mask)
-        put_panel(out_ref, 0, pair, *left)
-        put_panel(out_ref, half, pair, *right)
+        put_packed(pack_ref, pair, left + right)
+    out_ref[...] = pack_ref[...].astype(BF16)
 
 
 def early_kernel(
@@ -140,14 +176,26 @@
     scratch[...] = ref.astype(F32).reshape(scratch.shape)
 
 
-def triangle_kernel(panel_ref, out_ref, left_ref, right_ref, tri_ref):
-    peers, both, _ = panel_ref.shape
-    half = both // 2
+def spread_panels(panel_ref, pack_ref, left_ref, right_ref, chans):
+    peers = panel_ref.shape[0]
+    rows = left_ref.shape[0] // chans // peers
+    pack_ref[...] = panel_ref[...].astype(F32)
+    for pair in range(rows // 2):
+        blocks = get_packed(pack_ref, pair, rows // 2)
+        for n, block in enumerate(blocks):
+            side = left_ref if n < 2 else right_ref
+            i = 2 * pair + n % 2
+            for p in range(peers):
+                start = (p * rows + i) * chans
+                side[start : start + chans, :] = block[p * chans : (p + 1) * chans]
+
+
+def triangle_kernel(panel_ref, out_ref, left_ref, right_ref, tri_ref, pack_ref):
+    peers = panel_ref.shape[0]
     total = out_ref.shape[0] * out_ref.shape[1]
     chans = LANES // peers
     residues = total // chans
-    spread_rows(panel_ref[:, :half, :], left_ref)
-    spread_rows(panel_ref[:, half:, :], right_ref)
+    spread_panels(panel_ref, pack_ref, left_ref, right_ref, chans)
     for h in range(chans):
         rows = pl.ds(h, residues, stride=chans)
         left = left_ref[rows, :].astype(BF16)
@@ -202,13 +250,13 @@
     grads_ref[chans:] = out_sum
 
 
-def back_kernel(panel_ref, grad_ref, out_ref, left_ref, right_ref, tri_ref, left_out, right_out):
-    peers, both, _ = panel_ref.shape
-    half = both // 2
+def back_kernel(
+    panel_ref, grad_ref, out_ref, left_ref, right_ref, tri_ref, left_out, right_out, pack_ref
+):
+    peers = panel_ref.shape[0]
     chans = LANES // peers
     residues = left_ref.shape[0] // chans
-    spread_rows(panel_ref[:, :half, :], left_ref)
-    spread_rows(panel_ref[:, half:, :], right_ref)
+    spread_panels(panel_ref, pack_ref, left_ref, right_ref, chans)
     spread_rows(grad_ref[...], tri_ref)
     for h in range(chans):
         rows = pl.ds(h, residues, stride=chans)
@@ -218,9 +266,15 @@
         left_out[rows, :] = mat(grad.astype(BF16), right)
         turned = pad_rows(grad, LANES).T.astype(BF16)
         right_out[rows, :] = mat(turned, pad_rows(left, LANES))[:residues]
-    shape = (peers, half, LANES)
-    out_ref[:, :half, :] = left_out[...].astype(BF16).reshape(shape)
-    out_ref[:, half:, :] = right_out[...].astype(BF16).reshape(shape)
+    count = residues // peers
+    for pair in range(count // 2):
+        blocks = []
+        for side in (left_out, right_out):
+            for i in (2 * pair, 2 * pair + 1):
+                starts = [(p * count + i) * chans for p in range(peers)]
+                blocks.append(jnp.concatenate([side[s : s + chans, :] for s in starts], axis=0))
+        put_packed(pack_ref, pair, blocks)
+    out_ref[...] = pack_ref[...].astype(BF16)
 
 
 def grad_linear(factor_ref, i, left, right):
@@ -236,15 +290,14 @@
     )
 
 
-def proj_grad_kernel(back_ref, factor_ref, normed_ref, grads_ref, out_ref, rows_ref):
+def proj_grad_kernel(back_ref, factor_ref, normed_ref, grads_ref, out_ref, rows_ref, pack_ref):
     rows, wide, _ = factor_ref.shape
-    half = back_ref.shape[1] // 2
-    size = half // (rows // 2)
+    pack_ref[...] = back_ref[...].astype(F32)
     near, piece, _ = out_ref.shape
     proj_sum = jnp.zeros((wide, normed_ref.shape[2]), F32)
     for pair in range(rows // 2):
-        lefts = get_panel(back_ref, 0, pair, size)
-        rights = get_panel(back_ref, half, pair, size)
+        blocks = get_packed(pack_ref, pair, rows // 2)
+        lefts, rights = blocks[:2], blocks[2:]
         for i, left, right in zip((2 * pair, 2 * pair + 1), lefts, rights):
             proj_sum += mat(grad_linear(factor_ref, i, left, right), normed_ref[i])
     main = wide // near
@@ -258,17 +311,17 @@
 
 
 def pair_grad_kernel(
-    rep_ref, cot_ref, back_ref, factor_ref, grad_gate_ref, gain_ref, proj_ref, gate_ref, out_ref
+    rep_ref, cot_ref, back_ref, factor_ref, grad_gate_ref, gain_ref, proj_ref, gate_ref, out_ref,
+    pack_ref,
 ):
     rows, residues, _ = rep_ref.shape
-    half = back_ref.shape[1] // 2
-    size = half // (rows // 2)
+    pack_ref[...] = back_ref[...].astype(F32)
     proj = proj_ref[...]
     gate = gate_ref[...]
     gain = gain_ref[...]
     for pair in range(rows // 2):
-        lefts = get_panel(back_ref, 0, pair, size)
-        rights = get_panel(back_ref, half, pair, size)
+        blocks = get_packed(pack_ref, pair, rows // 2)
+        lefts, rights = blocks[:2], blocks[2:]
         for i, left, right in zip((2 * pair, 2 * pair + 1), lefts, rights):
             lin = grad_linear(factor_ref, i, left, right)
             grad = (mat(proj, lin) + mat(gate, grad_gate_ref[i])).T[:residues] * gain
@@ -318,8 +371,9 @@
             [pltpu.VMEM(a.shape, a.dtype) for a in args[smem:]]
             + [pltpu.SemaphoreType.DMA((len(args) - smem,))]
             if staged
-            else [pltpu.VMEM(shape, F32) for shape in scratch]
-        ),
+            else []
+        )
+        + [pltpu.VMEM(shape, F32) for shape in scratch],
         compiler_params=pltpu.CompilerParams(vmem_limit_bytes=LARGE_VMEM_BYTES if staged else VMEM_BYTES),
         cost_estimate=pl.CostEstimate(flops=flops, bytes_accessed=size, transcendentals=0),
     )(*args)
@@ -349,10 +403,11 @@
     info = lengths
     gain, gain_o = in_gain[None], out_gain[None]
     grid = (rows, LANES, LANES)
+    packed = (tiles, 2 * panel * 3 // 4, LANES)
 
     (panels,) = call(
-        panels_kernel, [((tiles, 2 * panel, LANES), BF16)], info, rep, gain, projections, smem=1,
-        staged=True,
+        panels_kernel, [(packed, BF16)], info, rep, gain, projections, smem=1, staged=True,
+        scratch=[packed],
     )
     sides = exchange(panels, "tile")
     normed, factor, sig, update, slope, upstream = call(
@@ -365,7 +420,8 @@
         flops=10**9,
     )
     (tri_chan,) = call(
-        triangle_kernel, [((tiles, panel, LANES), BF16)], sides, scratch=[(lines, LANES)] * 3
+        triangle_kernel, [((tiles, panel, LANES), BF16)], sides,
+        scratch=[(lines, LANES)] * 3 + [packed],
     )
     tri_rows = exchange(tri_chan, "tile")
     (grad_rows,) = call(
@@ -378,19 +434,18 @@
         rep, tri_rows, normed, sig, update, slope, gain_o, out_weight, flops=10**9,
     )
     (back,) = call(
-        back_kernel, [((tiles, 2 * panel, LANES), BF16)], sides, grad_chan,
-        scratch=[(lines, LANES)] * 5,
+        back_kernel, [(packed, BF16)], sides, grad_chan, scratch=[(lines, LANES)] * 5 + [packed],
     )
     back_rows = exchange(back, "tile")
     piece = -(-(wide + 2 * chans) // near // 16) * 16
     (pieces,) = call(
         proj_grad_kernel, [((near, piece, LANES), BF16)],
-        back_rows, factor, normed, grads, scratch=[(near * piece, LANES)],
+        back_rows, factor, normed, grads, scratch=[(near * piece, LANES), packed],
     )
     part = total(exchange(pieces, NEAR))
     (pair_grad,) = call(
         pair_grad_kernel, [(rep.shape, BF16)], rep, cot, back_rows, factor, grad_gate, gain,
-        projections, gate_weight, flops=10**9,
+        projections, gate_weight, flops=10**9, scratch=[packed],
     )
     whole = total(lax.all_gather(part, "zh"))
     sums = exchange(spread(whole, near), NEAR)

time: 139 us -> 138 us (level)
  transfers between devices with their start and end apart: 3 -> 3, of which waited for: 3 -> 3; matrix products, arithmetic and copies ran while one was open for 0% -> 0% of each run, Pallas kernels for 3% -> 4%
where the time goes in v5:
time: 138 us; the launch traced here: 137 us
  blocking collectives  85.3 us (62%)
  starting transfers between devices  19 us (14%)
  waiting for transfers between devices  15.6 us (11%)
  Pallas kernels  11.4 us (8%)
  local copies, waits for them, and re-layouts  4.24 us (3%)
  between operations  1.57 us (1%)
    all_to_all x3, blocking collectives, exchange(): return lax.all_to_all(pieces, axes, split_axis=0, concat_axis=0, tiled=True)  53.8 us
    all_gather x1, blocking collectives, body(): whole = total(lax.all_gather(part, 'zh'))  31.5 us
    all_to_all x3, starting transfers between devices, exchange(): return lax.all_to_all(pieces, axes, split_axis=0, concat_axis=0, tiled=True)  19 us
    all_to_all x3, waiting for transfers between devices, exchange(): return lax.all_to_all(pieces, axes, split_axis=0, concat_axis=0, tiled=True)  15.6 us
    pallas_call x9, Pallas kernels, call(): pl.pallas_call(kernel, out_shape=shapes, in_specs=[pl.BlockSpec(memory_sp...  11.4 us
    unnamed x22, local copies, waits for them, and re-layouts  3.51 us
  transfers between devices with their start and end apart: 3, of which 3 were waited for; matrix products, arithmetic and copies ran while one was open for 0% of the time, Pallas kernels for 4%

profile of v5, /device:TPU:1, one launch (start us, length us, event | category | flops | bytes accessed | tf_op | source)
XLA Modules:
  0.0 137.2 jit_solution(5480921855269263135)
XLA Ops:
  0.6 0.0 copy-start
  0.6 0.0 copy-start.4
  0.7 0.0 copy-start.1
  0.7 0.0 copy-start.3
  0.7 0.0 copy-start.2
  0.7 0.0 copy-start.5
  0.7 0.0 copy-start.6
  1.5 2.4 %shard_map.135 = bf16[16,72,128]{2,1,0:T(8,128)(2,1)} custom-call(s32[1]{0:T(128)S(6)} %copy.15.info_ref, bf16[6,96,128]{2,1,0:T(8,128)(2,1)} %bitcast.9, f32[1,128]{1,0:T(1,128)} %bitcast.13, bf16[128,512]{1,0:T(8,128)(2,1)} %proj_ref.5), custom_call_target="tpu_custom_call" | custom-call | bytes 279044 | tf_op jit(solution)/shard_map/pallas_call | solution.py:365
  3.9 15.1 %all_to_all.30.panel_ref = bf16[16,72,128]{2,1,0:T(8,128)(2,1)S(1)} all-to-all(bf16[16,72,128]{2,1,0:T(8,128)(2,1)} %shard_map.135), channel_id=1, replica_groups=mesh['zh'=16,'zl'=2,'core'=2,'tile'=16] {'tile'}, dimensions={0} | all-to-all | bytes 589824 | tf_op jit(solution)/shard_map/all_to_all | solution.py:383
  19.0 1.1 shard_map.136
  20.1 3.5 %all-to-all-start.1 = ((bf16[16,48,128]{2,1,0:T(8,128)(2,1)}), bf16[16,48,128]{2,1,0:T(8,128)(2,1)S(1)}, u32[]{:S(2)}, u32[]{:S(2)}) async-start(bf16[16,48,128]{2,1,0:T(8,128)(2,1)} %shard_map.136), calls=%async_computation.1 | async-start | bytes 393216 | tf_op jit(solution)/shard_map/all_to_all | solution.py:383
  23.6 0.0 copy-done
  23.6 0.0 copy-done.4
  23.6 0.0 copy-done.1
  23.6 0.0 copy-done.3
  23.7 0.0 copy-done.2
  23.7 0.0 copy-done.5
  23.7 0.0 copy-done.6
  23.7 1.2 shard_map.137
  24.9 0.0 copy-start.7
  25.0 0.7 copy-done.7
  25.7 0.0 copy-start.9
  25.7 0.8 copy-done.9
  26.4 4.2 %all-to-all-done.1.tri_ref = bf16[16,48,128]{2,1,0:T(8,128)(2,1)S(1)} async-done(((bf16[16,48,128]{2,1,0:T(8,128)(2,1)}), bf16[16,48,128]{2,1,0:T(8,128)(2,1)S(1)}, u32[]{:S(2)}, u32[]{:S(2)}) %all-to-all-start.1) | async-done | bytes 196640 | tf_op jit(solution)/shard_map/all_to_all | solution.py:383
  30.6 0.3 shard_map.139
  30.9 10.2 %all_to_all.31.grad_ref = bf16[16,48,128]{2,1,0:T(8,128)(2,1)S(1)} all-to-all(bf16[16,48,128]{2,1,0:T(8,128)(2,1)S(1)} %shard_map.139), channel_id=1, replica_groups=mesh['zh'=16,'zl'=2,'core'=2,'tile'=16] {'tile'}, dimensions={0} | all-to-all | bytes 393216 | tf_op jit(solution)/shard_map/all_to_all | solution.py:383
  41.1 1.3 shard_map.140
  42.4 3.6 %all-to-all-start.3 = ((bf16[16,72,128]{2,1,0:T(8,128)(2,1)}), bf16[16,72,128]{2,1,0:T(8,128)(2,1)S(1)}, u32[]{:S(2)}, u32[]{:S(2)}) async-start(bf16[16,72,128]{2,1,0:T(8,128)(2,1)} %shard_map.140), calls=%async_computation.3 | async-start | bytes 589824 | tf_op jit(solution)/shard_map/all_to_all | solution.py:383
  46.0 0.0 copy-start.8
  46.0 1.0 copy-done.8
  47.0 0.0 copy-start.10
  47.0 1.0 copy-done.10
  48.0 1.6 %shard_map.138 = (bf16[6,96,128]{2,1,0:T(8,128)(2,1)}, bf16[6,128,128]{2,1,0:T(8,128)(2,1)S(1)}, f32[256,128]{1,0:T(8,128)S(1)}) custom-call(bf16[6,96,128]{2,1,0:T(8,128)(2,1)S(1)} %bitcast.11, bf16[16,48,128]{2,1,0:T(8,128)(2,1)S(1)} %all-to-all-done.1.tri_ref, bf16[6,128,128]{2,1,0:T(8,128)(2,1)S(1)} %get-tuple-element.21.normed_ref, ...), custom_call_target="tpu_custom_call" | custom-call | flops 1000000000 | bytes 1556992 | tf_op jit(solution)/shard_map/pallas_call | solution.py:365
  49.6 4.1 %all-to-all-done.3.back_ref = bf16[16,72,128]{2,1,0:T(8,128)(2,1)S(1)} async-done(((bf16[16,72,128]{2,1,0:T(8,128)(2,1)}), bf16[16,72,128]{2,1,0:T(8,128)(2,1)S(1)}, u32[]{:S(2)}, u32[]{:S(2)}) %all-to-all-start.3) | async-done | bytes 294944 | tf_op jit(solution)/shard_map/all_to_all | solution.py:383
  53.6 0.5 shard_map.142
  54.2 28.5 %all_to_all.32 = bf16[64,16,128]{2,1,0:T(8,128)(2,1)S(1)} all-to-all(bf16[64,16,128]{2,1,0:T(8,128)(2,1)S(1)} %shard_map.142), channel_id=1, replica_groups=mesh['zh'=16,'zl'=2,'core'=2,'tile'=16] {'zl','core','tile'}, dimensions={0} | all-to-all | bytes 524288 | tf_op jit(solution)/shard_map/all_to_all | solution.py:383
  82.7 0.1 reduce_sum.24
  82.8 31.5 %all-gather = bf16[256,128]{1,0:T(8,128)(2,1)S(1)} all-gather(bf16[16,128]{1,0:T(8,128)(2,1)S(1)} %reduce_sum.24), channel_id=2, replica_groups=mesh['zh'=16,'zl'=2,'core'=2,'tile'=16] {'zh'}, dimensions={0}, use_global_device_ids=true | all-gather | bytes 69632 | tf_op jit(solution)/shard_map/all_gather | solution.py:450
  114.3 0.7 broadcast_in_dim.22
  115.0 11.9 %all-to-all-start.5 = ((bf16[64,16,128]{2,1,0:T(8,128)(2,1)}), bf16[64,16,128]{2,1,0:T(8,128)(2,1)S(1)}, u32[]{:S(2)}, u32[]{:S(2)}) async-start(bf16[64,16,128]{2,1,0:T(8,128)(2,1)} %broadcast_in_dim.22), calls=%async_computation.5 | async-start | bytes 524288 | tf_op jit(solution)/shard_map/all_to_all | solution.py:383
  126.9 2.0 %shard_map.141 = bf16[6,96,128]{2,1,0:T(8,128)(2,1)} custom-call(bf16[6,96,128]{2,1,0:T(8,128)(2,1)S(1)} %bitcast.12, bf16[6,96,128]{2,1,0:T(8,128)(2,1)S(1)} %bitcast.21, bf16[16,72,128]{2,1,0:T(8,128)(2,1)S(1)} %all-to-all-done.3.back_ref, f32[6,512,128]{2,1,0:T(8,128)S(1)} %get-tuple-element.27.factor_ref, ...), custom_call_target="tpu_custom_call" | custom-call | flops 1000000000 | bytes 2523648 | tf_op jit(solution)/shard_map/pallas_call | solution.py:365
  128.9 7.4 %all-to-all-done.5.sum_ref = bf16[64,16,128]{2,1,0:T(8,128)(2,1)S(1)} async-done(((bf16[64,16,128]{2,1,0:T(8,128)(2,1)}), bf16[64,16,128]{2,1,0:T(8,128)(2,1)S(1)}, u32[]{:S(2)}, u32[]{:S(2)}) %all-to-all-start.5) | async-done | bytes 262176 | tf_op jit(solution)/shard_map/all_to_all | solution.py:383
  136.2 0.9 shard_map.143
  (1 shorter events, 0.0 us)
Async XLA Ops:
  0.6 23.0 %copy-start = (bf16[128,512]{1,0:T(8,128)(2,1)S(1)}, bf16[128,512]{1,0:T(8,128)(2,1)}, u32[]{:S(2)}) copy-start(bf16[128,512]{1,0:T(8,128)(2,1)} %proj_ref.5) | copy-start | bytes 393220
  0.6 23.0 %copy-start.4 = (f32[128]{0:T(128)S(1)}, f32[128]{0:T(128)}, u32[]{:S(2)}) copy-start(f32[128]{0:T(128)} %param.11) | copy-start | bytes 1540
  0.7 23.0 %copy-start.1 = (bf16[1,6,96,128]{3,2,1,0:T(8,128)(2,1)S(1)}, bf16[1,6,96,128]{3,2,1,0:T(8,128)(2,1)}, u32[]{:S(2)}) copy-start(bf16[1,6,96,128]{3,2,1,0:T(8,128)(2,1)} %param.8) | copy-start | bytes 442372
  0.7 23.0 %copy-start.3 = (bf16[128,128]{1,0:T(8,128)(2,1)S(1)}, bf16[128,128]{1,0:T(8,128)(2,1)}, u32[]{:S(2)}) copy-start(bf16[128,128]{1,0:T(8,128)(2,1)} %out_weight_ref.5) | copy-start | bytes 98308
  0.7 23.0 %copy-start.2 = (bf16[128,128]{1,0:T(8,128)(2,1)S(1)}, bf16[128,128]{1,0:T(8,128)(2,1)}, u32[]{:S(2)}) copy-start(bf16[128,128]{1,0:T(8,128)(2,1)} %gate_ref.5) | copy-start | bytes 98308
  0.7 23.0 %copy-start.5 = (f32[128]{0:T(128)S(1)}, f32[128]{0:T(128)}, u32[]{:S(2)}) copy-start(f32[128]{0:T(128)} %param.14) | copy-start | bytes 1540
  0.7 23.0 %copy-start.6 = (bf16[1,6,96,128]{3,2,1,0:T(8,128)(2,1)S(1)}, bf16[1,6,96,128]{3,2,1,0:T(8,128)(2,1)}, u32[]{:S(2)}) copy-start(bf16[1,6,96,128]{3,2,1,0:T(8,128)(2,1)} %param.9) | copy-start | bytes 442372
  20.1 10.5 %all-to-all-start.1 = ((bf16[16,48,128]{2,1,0:T(8,128)(2,1)}), bf16[16,48,128]{2,1,0:T(8,128)(2,1)S(1)}, u32[]{:S(2)}, u32[]{:S(2)}) async-start(bf16[16,48,128]{2,1,0:T(8,128)(2,1)} %shard_map.136), calls=%async_computation.1 | async-start | bytes 393216 | tf_op jit(solution)/shard_map/all_to_all | solution.py:383
  24.9 0.7 copy-start.7
  25.7 0.8 copy-start.9
  42.4 11.2 %all-to-all-start.3 = ((bf16[16,72,128]{2,1,0:T(8,128)(2,1)}), bf16[16,72,128]{2,1,0:T(8,128)(2,1)S(1)}, u32[]{:S(2)}, u32[]{:S(2)}) async-start(bf16[16,72,128]{2,1,0:T(8,128)(2,1)} %shard_map.140), calls=%async_computation.3 | async-start | bytes 589824 | tf_op jit(solution)/shard_map/all_to_all | solution.py:383
  46.0 1.0 copy-start.8
  47.0 1.0 copy-start.10
  115.0 21.2 %all-to-all-start.5 = ((bf16[64,16,128]{2,1,0:T(8,128)(2,1)}), bf16[64,16,128]{2,1,0:T(8,128)(2,1)S(1)}, u32[]{:S(2)}, u32[]{:S(2)}) async-start(bf16[64,16,128]{2,1,0:T(8,128)(2,1)} %broadcast_in_dim.22), calls=%async_computation.5 | async-start | bytes 524288 | tf_op jit(solution)/shard_map/all_to_all | solution.py:383

commit v6 on v5

--- a/solution.py
+++ b/solution.py
@@ -332,6 +332,13 @@
             out_ref[i] = (cot_ref[i].astype(F32) + change).astype(BF16)
 
 
+def sum_kernel(parts_ref, out_ref):
+    whole = parts_ref[0].astype(F32)
+    for far in range(1, parts_ref.shape[0]):
+        whole += parts_ref[far].astype(F32)
+    out_ref[...] = jnp.broadcast_to(whole.astype(BF16)[None], out_ref.shape)
+
+
 def final_kernel(
     sum_ref, proj_ref, gate_ref, out_weight_ref, gain_ref, out_gain_ref,
     proj_grad_ref, gate_grad_ref, out_grad_ref, gain_grad_ref, out_gain_grad_ref, rows_ref,
@@ -447,8 +454,8 @@
         pair_grad_kernel, [(rep.shape, BF16)], rep, cot, back_rows, factor, grad_gate, gain,
         projections, gate_weight, flops=10**9, scratch=[packed],
     )
-    whole = total(lax.all_gather(part, "zh"))
-    sums = exchange(spread(whole, near), NEAR)
+    (whole,) = call(sum_kernel, [((near,) + part.shape, BF16)], lax.all_gather(part, "zh"))
+    sums = exchange(whole, NEAR)
     proj_grad, gate_grad, out_grad, gain_grad, gain_o_grad = call(
         final_kernel,
         [

time: 138 us -> 138 us (level)
    pallas_call x9 -> x10, Pallas kernels: 11.4 us -> 12.1 us  [call(): pl.pallas_call(kernel, out_shape=shapes, in_specs=[pl.BlockSpec(memory_sp...]
where the time goes in v6:
time: 138 us; the launch traced here: 137 us
  blocking collectives  85.3 us (62%)
  starting transfers between devices  19 us (14%)
  waiting for transfers between devices  15.6 us (11%)
  Pallas kernels  12.1 us (9%)
  local copies, waits for them, and re-layouts  3.5 us (3%)
  between operations  1.57 us (1%)
    all_to_all x3, blocking collectives, exchange(): return lax.all_to_all(pieces, axes, split_axis=0, concat_axis=0, tiled=True)  53.8 us
    all_gather x1, blocking collectives, body(): lax.all_gather(part, 'zh')  31.5 us
    all_to_all x3, starting transfers between devices, exchange(): return lax.all_to_all(pieces, axes, split_axis=0, concat_axis=0, tiled=True)  19 us
    all_to_all x3, waiting for transfers between devices, exchange(): return lax.all_to_all(pieces, axes, split_axis=0, concat_axis=0, tiled=True)  15.6 us
    pallas_call x10, Pallas kernels, call(): pl.pallas_call(kernel, out_shape=shapes, in_specs=[pl.BlockSpec(memory_sp...  12.1 us
    unnamed x22, local copies, waits for them, and re-layouts  3.5 us
  transfers between devices with their start and end apart: 3, of which 3 were waited for; matrix products, arithmetic and copies ran while one was open for 0% of the time, Pallas kernels for 4%

profile of v6, /device:TPU:1, one launch (start us, length us, event | category | flops | bytes accessed | tf_op | source)
XLA Modules:
  0.0 137.1 jit_solution(13639372219194853880)
XLA Ops:
  0.6 0.0 copy-start
  0.6 0.0 copy-start.4
  0.7 0.0 copy-start.1
  0.7 0.0 copy-start.3
  0.7 0.0 copy-start.2
  0.7 0.0 copy-start.5
  0.7 0.0 copy-start.6
  1.5 2.4 %shard_map.135 = bf16[16,72,128]{2,1,0:T(8,128)(2,1)} custom-call(s32[1]{0:T(128)S(6)} %copy.15.info_ref, bf16[6,96,128]{2,1,0:T(8,128)(2,1)} %bitcast.10, f32[1,128]{1,0:T(1,128)} %bitcast.14, bf16[128,512]{1,0:T(8,128)(2,1)} %proj_ref.5), custom_call_target="tpu_custom_call" | custom-call | bytes 279044 | tf_op jit(solution)/shard_map/pallas_call | solution.py:372
  3.9 15.1 %all_to_all.30.panel_ref = bf16[16,72,128]{2,1,0:T(8,128)(2,1)S(1)} all-to-all(bf16[16,72,128]{2,1,0:T(8,128)(2,1)} %shard_map.135), channel_id=1, replica_groups=mesh['zh'=16,'zl'=2,'core'=2,'tile'=16] {'tile'}, dimensions={0} | all-to-all | bytes 589824 | tf_op jit(solution)/shard_map/all_to_all | solution.py:390
  19.0 1.1 shard_map.136
  20.1 3.5 %all-to-all-start.1 = ((bf16[16,48,128]{2,1,0:T(8,128)(2,1)}), bf16[16,48,128]{2,1,0:T(8,128)(2,1)S(1)}, u32[]{:S(2)}, u32[]{:S(2)}) async-start(bf16[16,48,128]{2,1,0:T(8,128)(2,1)} %shard_map.136), calls=%async_computation.1 | async-start | bytes 393216 | tf_op jit(solution)/shard_map/all_to_all | solution.py:390
  23.6 0.0 copy-done
  23.6 0.0 copy-done.4
  23.6 0.0 copy-done.1
  23.7 0.0 copy-done.3
  23.7 0.0 copy-done.2
  23.7 0.0 copy-done.5
  23.7 0.0 copy-done.6
  23.7 1.2 shard_map.137
  24.9 0.0 copy-start.7
  25.0 0.7 copy-done.7
  25.7 0.0 copy-start.9
  25.7 0.7 copy-done.9
  26.4 4.2 %all-to-all-done.1.tri_ref = bf16[16,48,128]{2,1,0:T(8,128)(2,1)S(1)} async-done(((bf16[16,48,128]{2,1,0:T(8,128)(2,1)}), bf16[16,48,128]{2,1,0:T(8,128)(2,1)S(1)}, u32[]{:S(2)}, u32[]{:S(2)}) %all-to-all-start.1) | async-done | bytes 196640 | tf_op jit(solution)/shard_map/all_to_all | solution.py:390
  30.6 0.3 shard_map.139
  30.9 10.2 %all_to_all.31.grad_ref = bf16[16,48,128]{2,1,0:T(8,128)(2,1)S(1)} all-to-all(bf16[16,48,128]{2,1,0:T(8,128)(2,1)S(1)} %shard_map.139), channel_id=1, replica_groups=mesh['zh'=16,'zl'=2,'core'=2,'tile'=16] {'tile'}, dimensions={0} | all-to-all | bytes 393216 | tf_op jit(solution)/shard_map/all_to_all | solution.py:390
  41.1 1.3 shard_map.140
  42.4 3.6 %all-to-all-start.3 = ((bf16[16,72,128]{2,1,0:T(8,128)(2,1)}), bf16[16,72,128]{2,1,0:T(8,128)(2,1)S(1)}, u32[]{:S(2)}, u32[]{:S(2)}) async-start(bf16[16,72,128]{2,1,0:T(8,128)(2,1)} %shard_map.140), calls=%async_computation.3 | async-start | bytes 589824 | tf_op jit(solution)/shard_map/all_to_all | solution.py:390
  46.0 0.0 copy-start.8
  46.0 1.0 copy-done.8
  47.0 0.0 copy-start.10
  47.0 1.0 copy-done.10
  48.0 1.6 %shard_map.138 = (bf16[6,96,128]{2,1,0:T(8,128)(2,1)}, bf16[6,128,128]{2,1,0:T(8,128)(2,1)S(1)}, f32[256,128]{1,0:T(8,128)S(1)}) custom-call(bf16[6,96,128]{2,1,0:T(8,128)(2,1)S(1)} %bitcast.12, bf16[16,48,128]{2,1,0:T(8,128)(2,1)S(1)} %all-to-all-done.1.tri_ref, bf16[6,128,128]{2,1,0:T(8,128)(2,1)S(1)} %get-tuple-element.21.normed_ref, ...), custom_call_target="tpu_custom_call" | custom-call | flops 1000000000 | bytes 1556992 | tf_op jit(solution)/shard_map/pallas_call | solution.py:372
  49.6 4.1 %all-to-all-done.3.back_ref = bf16[16,72,128]{2,1,0:T(8,128)(2,1)S(1)} async-done(((bf16[16,72,128]{2,1,0:T(8,128)(2,1)}), bf16[16,72,128]{2,1,0:T(8,128)(2,1)S(1)}, u32[]{:S(2)}, u32[]{:S(2)}) %all-to-all-start.3) | async-done | bytes 294944 | tf_op jit(solution)/shard_map/all_to_all | solution.py:390
  53.6 0.5 shard_map.142
  54.2 28.5 %all_to_all.32 = bf16[64,16,128]{2,1,0:T(8,128)(2,1)S(1)} all-to-all(bf16[64,16,128]{2,1,0:T(8,128)(2,1)S(1)} %shard_map.142), channel_id=1, replica_groups=mesh['zh'=16,'zl'=2,'core'=2,'tile'=16] {'zl','core','tile'}, dimensions={0} | all-to-all | bytes 524288 | tf_op jit(solution)/shard_map/all_to_all | solution.py:390
  82.7 0.1 reduce_sum.12
  82.8 31.5 %all-gather = bf16[256,128]{1,0:T(8,128)(2,1)S(1)} all-gather(bf16[16,128]{1,0:T(8,128)(2,1)S(1)} %reduce_sum.12), channel_id=2, replica_groups=mesh['zh'=16,'zl'=2,'core'=2,'tile'=16] {'zh'}, dimensions={0}, use_global_device_ids=true | all-gather | bytes 69632 | tf_op jit(solution)/shard_map/all_gather | solution.py:457
  114.3 0.7 shard_map.143
  115.0 11.9 %all-to-all-start.5 = ((bf16[64,16,128]{2,1,0:T(8,128)(2,1)}), bf16[64,16,128]{2,1,0:T(8,128)(2,1)S(1)}, u32[]{:S(2)}, u32[]{:S(2)}) async-start(bf16[64,16,128]{2,1,0:T(8,128)(2,1)} %shard_map.143), calls=%async_computation.5 | async-start | bytes 524288 | tf_op jit(solution)/shard_map/all_to_all | solution.py:390
  126.9 2.0 %shard_map.141 = bf16[6,96,128]{2,1,0:T(8,128)(2,1)} custom-call(bf16[6,96,128]{2,1,0:T(8,128)(2,1)S(1)} %bitcast.13, bf16[6,96,128]{2,1,0:T(8,128)(2,1)S(1)} %bitcast.22, bf16[16,72,128]{2,1,0:T(8,128)(2,1)S(1)} %all-to-all-done.3.back_ref, f32[6,512,128]{2,1,0:T(8,128)S(1)} %get-tuple-element.27.factor_ref, ...), custom_call_target="tpu_custom_call" | custom-call | flops 1000000000 | bytes 2523648 | tf_op jit(solution)/shard_map/pallas_call | solution.py:372
  128.9 7.4 %all-to-all-done.5.sum_ref = bf16[64,16,128]{2,1,0:T(8,128)(2,1)S(1)} async-done(((bf16[64,16,128]{2,1,0:T(8,128)(2,1)}), bf16[64,16,128]{2,1,0:T(8,128)(2,1)S(1)}, u32[]{:S(2)}, u32[]{:S(2)}) %all-to-all-start.5) | async-done | bytes 262176 | tf_op jit(solution)/shard_map/all_to_all | solution.py:390
  136.2 0.9 shard_map.144
Async XLA Ops:
  0.6 23.0 %copy-start = (bf16[128,512]{1,0:T(8,128)(2,1)S(1)}, bf16[128,512]{1,0:T(8,128)(2,1)}, u32[]{:S(2)}) copy-start(bf16[128,512]{1,0:T(8,128)(2,1)} %proj_ref.5) | copy-start | bytes 393220
  0.6 23.0 %copy-start.4 = (f32[128]{0:T(128)S(1)}, f32[128]{0:T(128)}, u32[]{:S(2)}) copy-start(f32[128]{0:T(128)} %param.11) | copy-start | bytes 1540
  0.7 23.0 %copy-start.1 = (bf16[1,6,96,128]{3,2,1,0:T(8,128)(2,1)S(1)}, bf16[1,6,96,128]{3,2,1,0:T(8,128)(2,1)}, u32[]{:S(2)}) copy-start(bf16[1,6,96,128]{3,2,1,0:T(8,128)(2,1)} %param.8) | copy-start | bytes 442372
  0.7 23.0 %copy-start.3 = (bf16[128,128]{1,0:T(8,128)(2,1)S(1)}, bf16[128,128]{1,0:T(8,128)(2,1)}, u32[]{:S(2)}) copy-start(bf16[128,128]{1,0:T(8,128)(2,1)} %out_weight_ref.5) | copy-start | bytes 98308
  0.7 23.0 %copy-start.2 = (bf16[128,128]{1,0:T(8,128)(2,1)S(1)}, bf16[128,128]{1,0:T(8,128)(2,1)}, u32[]{:S(2)}) copy-start(bf16[128,128]{1,0:T(8,128)(2,1)} %gate_ref.5) | copy-start | bytes 98308
  0.7 23.0 %copy-start.5 = (f32[128]{0:T(128)S(1)}, f32[128]{0:T(128)}, u32[]{:S(2)}) copy-start(f32[128]{0:T(128)} %param.14) | copy-start | bytes 1540
  0.7 23.0 %copy-start.6 = (bf16[1,6,96,128]{3,2,1,0:T(8,128)(2,1)S(1)}, bf16[1,6,96,128]{3,2,1,0:T(8,128)(2,1)}, u32[]{:S(2)}) copy-start(bf16[1,6,96,128]{3,2,1,0:T(8,128)(2,1)} %param.9) | copy-start | bytes 442372
  20.1 10.5 %all-to-all-start.1 = ((bf16[16,48,128]{2,1,0:T(8,128)(2,1)}), bf16[16,48,128]{2,1,0:T(8,128)(2,1)S(1)}, u32[]{:S(2)}, u32[]{:S(2)}) async-start(bf16[16,48,128]{2,1,0:T(8,128)(2,1)} %shard_map.136), calls=%async_computation.1 | async-start | bytes 393216 | tf_op jit(solution)/shard_map/all_to_all | solution.py:390
  24.9 0.8 copy-start.7
  25.7 0.7 copy-start.9
  42.4 11.2 %all-to-all-start.3 = ((bf16[16,72,128]{2,1,0:T(8,128)(2,1)}), bf16[16,72,128]{2,1,0:T(8,128)(2,1)S(1)}, u32[]{:S(2)}, u32[]{:S(2)}) async-start(bf16[16,72,128]{2,1,0:T(8,128)(2,1)} %shard_map.140), calls=%async_computation.3 | async-start | bytes 589824 | tf_op jit(solution)/shard_map/all_to_all | solution.py:390
  46.0 1.0 copy-start.8
  47.0 1.0 copy-start.10
  115.0 21.2 %all-to-all-start.5 = ((bf16[64,16,128]{2,1,0:T(8,128)(2,1)}), bf16[64,16,128]{2,1,0:T(8,128)(2,1)S(1)}, u32[]{:S(2)}, u32[]{:S(2)}) async-start(bf16[64,16,128]{2,1,0:T(8,128)(2,1)} %shard_map.143), calls=%async_computation.5 | async-start | bytes 524288 | tf_op jit(solution)/shard_map/all_to_all | solution.py:390
